TPU v7x, 256 devices: a whole 4x4x8 slice. The times are simulated.
256 devices in a mesh: gx: 8 (over x, core), gy: 32 (over y, z).
Axes of the slice: x: 4, y: 4, z: 8, core: 2. Of those that a mesh axis runs over, the one named last changes fastest.
Arguments:
- salinity: float32 [4, 2048, 8192], P(None, 'gx', 'gy'), may hold values from -8 to 8, as said below
Outputs:
- decomposed: float32 [4, 2048, 8192], P(None, 'gx', 'gy')
Inputs may be any that keep to these rules, and one draw needn't show every extreme that they name: salinity anomaly of a cell, in practical salinity units.
All inputs are finite; a program needn't handle non-finite values.
Results may differ from a plain program's by a relative error of at most 0.0003.
Values sent between devices are 32-bit elements; how exact they have to be, the bound alone decides.
A program may use at most 128 MiB of HBM per device.

v0:
```python
import jax
import jax.numpy as jnp
import numpy as np
from jax import lax
from jax.sharding import PartitionSpec as P

LEVELS = 3


smooth_length = 64.0


def padded_2(x, sides, width):
    for axis, dim in sides:
        devices, length = (lax.axis_size(axis), x.shape[dim])
        up = [(i, (i + 1) % devices) for i in range(devices - 1)]
        down = [(j, i) for i, j in up]
        last = lax.slice_in_dim(x, length - width, length, axis=dim)
        initial = lax.slice_in_dim(x, 0, width, axis=dim)
        before = lax.ppermute(last, axis, up)
        after = lax.ppermute(initial, axis, down)
        x = jnp.concatenate([before, x, after], axis=dim)
    return x


def line_constants():
    square = smooth_length * smooth_length
    off_size = square - 1.0 / 3.0
    inner_diag = (4.0 / 3.0 + 2.0 * square) / off_size
    end_diag = (2.0 / 3.0 + square) / off_size
    return (inner_diag, end_diag, square / (off_size * off_size))


def pivots(count):
    inner_diag, end_diag, _ = line_constants()
    entries = [end_diag]
    for position in range(1, count):
        diagonal = end_diag if position == count - 1 else inner_diag
        entries.append(diagonal - 1.0 / entries[-1])
    return np.array(entries)


def checker(row_ids, col_ids):
    parity = (row_ids[:, None] + col_ids[None, :]) % 2
    return 1.0 - 2.0 * parity.astype(jnp.float32)


def shaped(vector, axis, rank_count):
    target = [1] * rank_count
    target[axis] = -1
    return vector.reshape(target)


def interpolate(field, axis, count, start, total):
    middle = lax.slice_in_dim(field, 1, count + 2, axis=axis)
    before = lax.slice_in_dim(field, 0, count + 1, axis=axis)
    after = lax.slice_in_dim(field, 2, count + 3, axis=axis)
    places = jnp.arange(1, count + 2, dtype=jnp.int32)
    global_ids = start + places - 2
    last_node = global_ids == total - 1
    w_left = jnp.where(last_node, 1.0, 0.5).astype(jnp.float32)
    w_right = jnp.where(last_node, 0.0, 0.5).astype(jnp.float32)
    is_odd = places % 2 == 1
    blended = shaped(w_left, axis, field.ndim) * before + shaped(w_right, axis, field.ndim) * after
    inner = jnp.where(shaped(is_odd, axis, field.ndim), blended, middle)
    head = lax.slice_in_dim(field, 0, 1, axis=axis)
    tail = lax.slice_in_dim(field, count + 2, count + 3, axis=axis)
    return jnp.concatenate([head, inner, tail], axis=axis)


def valid_mask(count, start, total):
    global_ids = start + jnp.arange(count + 3, dtype=jnp.int32) - 2
    return ((global_ids >= 0) & (global_ids < total)).astype(jnp.float32)


def restrict(field, axis, count, start, total):
    global_ids = start + jnp.arange(count + 1, dtype=jnp.int32) - 1
    weight = jnp.where((global_ids == 0) | (global_ids == total - 1), 2.0, 4.0).astype(jnp.float32)
    mass = (
        lax.slice_in_dim(field, 0, count + 1, axis=axis)
        + shaped(weight, axis, field.ndim) * lax.slice_in_dim(field, 1, count + 2, axis=axis)
        + lax.slice_in_dim(field, 2, count + 3, axis=axis)
    ) / 6.0
    centre = lax.slice_in_dim(mass, 1, count + 1, 2, axis=axis)
    lower = lax.slice_in_dim(mass, 0, count, 2, axis=axis)
    upper = lax.slice_in_dim(mass, 2, count + 1, 2, axis=axis)
    coarse_ids = start // 2 + jnp.arange(count // 2, dtype=jnp.int32)
    w_lower = jnp.where(coarse_ids == 0, 0.0, 0.5).astype(jnp.float32)
    w_upper = jnp.where(2 * coarse_ids + 1 == total - 1, 1.0, 0.5).astype(jnp.float32)
    return (
        centre
        + shaped(w_lower, axis, field.ndim) * lower
        + shaped(w_upper, axis, field.ndim) * upper
    )


def level_terms(
    halo_field, ax_rows, ax_cols, row_count, col_count, row_start, col_start, row_total, col_total
):
    window = lax.slice_in_dim(halo_field, 0, row_count + 3, axis=ax_rows)
    window = lax.slice_in_dim(window, 0, col_count + 3, axis=ax_cols)
    along_cols = interpolate(window, ax_cols, col_count, col_start, col_total)
    interpolant = interpolate(along_cols, ax_rows, row_count, row_start, row_total)
    masking = shaped(valid_mask(row_count, row_start, row_total), ax_rows, window.ndim) * shaped(
        valid_mask(col_count, col_start, col_total), ax_cols, window.ndim
    )
    detail = (window - interpolant) * masking
    load = restrict(detail, ax_rows, row_count, row_start, row_total)
    load = restrict(load, ax_cols, col_count, col_start, col_total)
    own = lax.slice_in_dim(detail, 2, row_count + 2, axis=ax_rows)
    own = lax.slice_in_dim(own, 2, col_count + 2, axis=ax_cols)
    coarse = lax.slice_in_dim(halo_field, 2, row_count + 2, 2, axis=ax_rows)
    coarse = lax.slice_in_dim(coarse, 2, col_count + 2, 2, axis=ax_cols)
    return (own, coarse, load)


def sweep_numpy(piece, length):
    lower_sum = np.cumsum(piece[:length])
    upper_sum = np.concatenate([np.zeros(1), np.cumsum(piece[1:])])
    row_ids = np.arange(length)[:, None]
    col_ids = np.arange(length)[None, :]
    parity = 1.0 - 2.0 * ((row_ids - col_ids) % 2)
    below = col_ids <= row_ids
    gap_down = np.where(below, lower_sum[:, None] - lower_sum[None, :], 0.0)
    forward_tab = np.where(below, parity * np.exp(-gap_down), 0.0)
    positions = np.arange(length)
    forward_in = (1.0 - 2.0 * ((positions + 1) % 2)) * np.exp(-lower_sum)
    above = col_ids >= row_ids
    gap_up = np.where(above, upper_sum[None, 1:] - upper_sum[:length, None], 0.0)
    backward_tab = np.where(above, parity * np.exp(-gap_up), 0.0)
    backward_in = (1.0 - 2.0 * ((length - positions) % 2)) * np.exp(
        -(upper_sum[length] - upper_sum[:length])
    )
    return (forward_tab, forward_in, backward_tab, backward_in)


def stacked_tables(total, pieces):
    length = total // pieces
    logs = np.concatenate([np.zeros(1), np.log(pivots(total))])
    tables = [
        sweep_numpy(logs[begin : begin + length + 1], length) for begin in range(0, total, length)
    ]
    return tuple(
        (
            jnp.asarray(np.stack([entry[member] for entry in tables]), jnp.float32)
            for member in range(4)
        )
    )


def compose(earlier, later):
    return (earlier[0] * later[0], later[0] * earlier[1] + later[1])


def full_rows(block):
    pieces = lax.axis_size("gx")
    length = block.shape[1] // pieces
    f_tab, f_in, b_tab, b_in = stacked_tables(block.shape[1], pieces)
    split_block = block.reshape(block.shape[0], pieces, length, block.shape[2])
    partial_f = jnp.einsum("sik,dskb->dsib", f_tab, split_block, precision=lax.Precision.HIGHEST)
    _, ends = lax.associative_scan(
        compose, (f_in[:, length - 1].reshape(1, pieces, 1), partial_f[:, :, length - 1, :]), axis=1
    )
    entering = jnp.concatenate([jnp.zeros_like(ends[:, :1]), ends[:, :-1]], axis=1)
    forward = partial_f + f_in[None, :, :, None] * entering[:, :, None, :]
    partial_b = jnp.einsum("sik,dskb->dsib", b_tab, forward, precision=lax.Precision.HIGHEST)
    _, heads = lax.associative_scan(
        compose, (b_in[:, 0].reshape(1, pieces, 1), partial_b[:, :, 0, :]), reverse=True, axis=1
    )
    leaving = jnp.concatenate([heads[:, 1:], jnp.zeros_like(heads[:, :1])], axis=1)
    solved = (partial_b + b_in[None, :, :, None] * leaving[:, :, None, :]).reshape(block.shape)
    return lax.all_to_all(solved, "gx", split_axis=1, concat_axis=2, tiled=True)


def full_cols(block):
    pieces = lax.axis_size("gy")
    length = block.shape[2] // pieces
    f_tab, f_in, b_tab, b_in = stacked_tables(block.shape[2], pieces)
    split_block = block.reshape(block.shape[0], block.shape[1], pieces, length)
    partial_f = jnp.einsum("sik,dask->dasi", f_tab, split_block, precision=lax.Precision.HIGHEST)
    _, ends = lax.associative_scan(
        compose, (f_in[:, length - 1].reshape(1, 1, pieces), partial_f[:, :, :, length - 1]), axis=2
    )
    entering = jnp.concatenate([jnp.zeros_like(ends[:, :, :1]), ends[:, :, :-1]], axis=2)
    forward = partial_f + f_in[None, None, :, :] * entering[:, :, :, None]
    partial_b = jnp.einsum("sik,dask->dasi", b_tab, forward, precision=lax.Precision.HIGHEST)
    _, heads = lax.associative_scan(
        compose, (b_in[:, 0].reshape(1, 1, pieces), partial_b[:, :, :, 0]), reverse=True, axis=2
    )
    leaving = jnp.concatenate([heads[:, :, 1:], jnp.zeros_like(heads[:, :, :1])], axis=2)
    solved = (partial_b + b_in[None, None, :, :] * leaving[:, :, :, None]).reshape(block.shape)
    return lax.all_to_all(solved, "gy", split_axis=2, concat_axis=1, tiled=True)


def assemble(own, coarse_values):
    depth, row_count, col_count = own.shape
    half = coarse_values.shape[2]
    spread_table = (np.arange(col_count)[None, :] == 2 * np.arange(half)[:, None]).astype(
        np.float32
    )
    spread = jnp.einsum(
        "drh,hw->drw", coarse_values, jnp.asarray(spread_table), precision=lax.Precision.HIGHEST
    )
    paired = own.reshape(depth, row_count // 2, 2, col_count)
    even_cols = jnp.arange(col_count, dtype=jnp.int32) % 2 == 0
    merged = jnp.where(even_cols[None, None, :], spread, paired[:, :, 0, :])
    return jnp.stack([merged, paired[:, :, 1, :]], axis=2).reshape(depth, row_count, col_count)


def shards(salinity):
    _, _, line_factor = line_constants()
    nodes = salinity
    details = []
    for level_step in range(LEVELS):
        row_count = nodes.shape[1]
        col_count = nodes.shape[2]
        padded = padded_2(nodes, (("gx", 1), ("gy", 2)), 2)
        row_start = lax.axis_index("gx") * row_count
        col_start = lax.axis_index("gy") * col_count
        own, coarse, load = level_terms(
            padded,
            1,
            2,
            row_count,
            col_count,
            row_start,
            col_start,
            row_count * lax.axis_size("gx"),
            col_count * lax.axis_size("gy"),
        )
        coarse_rows = row_start // 2 + jnp.arange(row_count // 2, dtype=jnp.int32)
        coarse_cols = col_start // 2 + jnp.arange(col_count // 2, dtype=jnp.int32)
        signs = checker(coarse_rows, coarse_cols)[None, :, :]
        scaled = line_factor * signs * load
        across = full_rows(lax.all_to_all(scaled, "gx", split_axis=2, concat_axis=1, tiled=True))
        solved = full_cols(lax.all_to_all(across, "gy", split_axis=1, concat_axis=2, tiled=True))
        solved = signs * solved
        details.append(own)
        nodes = coarse + solved
    field = nodes
    for own in reversed(details):
        field = assemble(own, field)
    return field


def solution(mesh):
    placed = (P(None, "gx", "gy"),)
    return jax.shard_map(
        shards, mesh=mesh, in_specs=placed, out_specs=P(None, "gx", "gy"), check_vma=False
    )
```

profile of v0, /device:TPU:1, one launch (start us, length us, event | category | flops | bytes accessed | tf_op | source)
XLA Modules:
  0.0 422.1 jit_solution(12381796459729535163)
XLA Ops:
  0.8 5.1 %collective-permute-start.1 = (f32[4,2,256]{2,1,0:T(2,128)S(1)}, f32[4,2,256]{2,1,0:T(2,128)S(1)}, u32[]{:S(2)}, u32[]{:S(2)}) collective-permute-start(f32[4,2,256]{2,1,0:T(2,128)S(1)} %get-tuple-element.10), channel_id=1, source_target_pairs={{32,0},{64,32},{96,64},{128,96},{160,128},{192,160},{224,192},{33,... | collective-permute-start | bytes 24584 | tf_op jit(solution)/shard_map/ppermute | solution.py:21
  11.4 3.0 collective-permute-start.2
  16.3 3.4 collective-permute-done.3
  32.7 8.8 %slice.1615 = f32[4,128,128]{2,1,0:T(8,128)S(1)} slice(f32[4,128,257]{2,1,0:T(8,128)S(1)} %fusion.16), slice={[0:4:1], [0:128:1], [2:257:2]} | slice | bytes 524288 | tf_op jit(solution)/shard_map/slice | solution.py:86
  41.5 8.8 %slice.1613 = f32[4,128,128]{2,1,0:T(8,128)S(1)} slice(f32[4,128,257]{2,1,0:T(8,128)S(1)} %fusion.16), slice={[0:4:1], [0:128:1], [1:257:2]} | slice | bytes 524288 | tf_op jit(solution)/shard_map/slice | solution.py:84
  50.3 8.8 %slice.1614 = f32[4,128,128]{2,1,0:T(8,128)S(1)} slice(f32[4,128,257]{2,1,0:T(8,128)S(1)} %fusion.16), slice={[0:4:1], [0:128:1], [0:256:2]} | slice | bytes 524288 | tf_op jit(solution)/shard_map/slice | solution.py:85
  60.1 5.6 %all-to-all-start = ((f32[4,128,128]{1,0,2:T(4,128)}), f32[4,128,128]{1,0,2:T(4,128)S(1)}, u32[]{:S(2)}, u32[]{:S(2)}) async-start(f32[4,128,128]{1,0,2:T(4,128)} %copy.310), calls=%async_computation | async-start | bytes 524288 | tf_op jit(solution)/shard_map/all_to_all | solution.py:235
  66.8 5.3 %all-to-all-done = f32[4,128,128]{1,0,2:T(4,128)S(1)} async-done(((f32[4,128,128]{1,0,2:T(4,128)}), f32[4,128,128]{1,0,2:T(4,128)S(1)}, u32[]{:S(2)}, u32[]{:S(2)}) %all-to-all-start) | async-done | bytes 262176 | tf_op jit(solution)/shard_map/all_to_all | solution.py:235
  79.6 3.8 reshape.935
  83.3 4.4 %all-to-all-start.1 = ((f32[8,1,8192]{2,1,0:T(1,128)}), f32[8,1,8192]{2,1,0:T(1,128)S(1)}, u32[]{:S(2)}, u32[]{:S(2)}) async-start(f32[8,1,8192]{2,1,0:T(1,128)} %reshape.935), calls=%async_computation.1 | async-start | bytes 524288 | tf_op jit(solution)/shard_map/all_to_all | solution.py:172
  87.7 6.5 %all-to-all-done.1 = f32[8,1,8192]{2,1,0:T(1,128)S(1)} async-done(((f32[8,1,8192]{2,1,0:T(1,128)}), f32[8,1,8192]{2,1,0:T(1,128)S(1)}, u32[]{:S(2)}, u32[]{:S(2)}) %all-to-all-start.1) | async-done | bytes 262176 | tf_op jit(solution)/shard_map/all_to_all | solution.py:172
  95.9 2.8 reshape.936
  101.4 11.5 %all-to-all-start.2 = ((f32[4,128,128]{2,0,1:T(4,128)}), f32[4,128,128]{2,0,1:T(4,128)S(1)}, u32[]{:S(2)}, u32[]{:S(2)}) async-start(f32[4,128,128]{2,0,1:T(4,128)} %copy.321), calls=%async_computation.2 | async-start | bytes 524288 | tf_op jit(solution)/shard_map/all_to_all | solution.py:236
  114.3 8.3 %all-to-all-done.2 = f32[4,128,128]{2,0,1:T(4,128)S(1)} async-done(((f32[4,128,128]{2,0,1:T(4,128)}), f32[4,128,128]{2,0,1:T(4,128)S(1)}, u32[]{:S(2)}, u32[]{:S(2)}) %all-to-all-start.2) | async-done | bytes 262176 | tf_op jit(solution)/shard_map/all_to_all | solution.py:236
  122.5 5.1 %convolution_bitcast_fusion.1 = f32[4,4,32,128]{3,1,0,2:T(4,128)S(1)} fusion(f32[32,128,128,1]{2,1,3,0:T(8,128)} %constant.863, f32[4,32,4,128]{3,0,2,1:T(4,128)S(1)} %bitcast.243), kind=kOutput, calls=%fused_computation.36 | convolution fusion | flops 100663296 | bytes 2621440 | tf_op jit(solution)/shard_map/sik,dask->dasi/dot_general | solution.py:180
  133.0 5.1 %convolution_bitcast_fusion = f32[4,4,32,128]{3,1,0,2:T(4,128)S(1)} fusion(f32[32,128,128,1]{2,1,3,0:T(8,128)} %constant.864, f32[4,4,32,128]{3,1,0,2:T(4,128)S(1)} %convolution_bitcast_fusion.1, f32[4,4,32]{1,0,2:T(4,128)S(1)} %concatenate.217.clone, f32[32,128]{1,0:T(8,128)S(1)} %copy-done.16), kind=kOutput, calls=%fused_computation.35 | convolution fusion | flops 100794368 | bytes 2639872 | tf_op jit(solution)/shard_map/sik,dask->dasi/dot_general | solution.py:186
  143.8 6.0 %copy.398 = f32[4,4,32,128]{1,0,3,2:T(4,128)} copy(f32[4,4,32,128]{3,1,0,2:T(4,128)S(1)} %multiply_add_fusion.3) | data formatting | bytes 524288 | tf_op jit(solution)/shard_map/reshape | solution.py:191
  149.8 11.9 %reshape.937 = f32[32,1,2048]{2,1,0:T(1,128)} reshape(f32[4096,4,4]{2,1,0:T(4,128)} %bitcast.218) | data formatting | bytes 524288
  161.7 6.2 %all-to-all-start.3 = ((f32[32,1,2048]{2,1,0:T(1,128)}), f32[32,1,2048]{2,1,0:T(1,128)S(1)}, u32[]{:S(2)}, u32[]{:S(2)}) async-start(f32[32,1,2048]{2,1,0:T(1,128)} %reshape.937), calls=%async_computation.3 | async-start | bytes 524288 | tf_op jit(solution)/shard_map/all_to_all | solution.py:192
  171.1 8.8 %slice.1592 = f32[4,128,128]{2,1,0:T(8,128)S(1)} slice(f32[4,128,260]{2,1,0:T(8,128)S(1)} %slice.1591), slice={[0:4:1], [0:128:1], [2:258:2]} | slice | bytes 524288 | tf_op jit(solution)/shard_map/slice | solution.py:113
  181.1 12.3 %reshape.938 = f32[4096,4,4]{2,1,0:T(4,128)} reshape(f32[32,2048]{1,0:T(8,128)S(1)} %reduce.1) | data formatting | bytes 524288
  193.4 6.7 %copy.330 = f32[4,4,32,128]{3,1,2,0:T(4,128)S(1)} copy(f32[4,4,32,128]{1,0,3,2:T(4,128)} %bitcast.219) | data formatting | bytes 524288 | tf_op jit(solution)/shard_map/all_to_all | solution.py:192
  200.2 4.0 collective-permute-start.5
  207.4 3.5 collective-permute-start.6
  212.3 4.6 %collective-permute-done.6 = f32[4,132,2]{2,1,0:T(8,128)S(1)} collective-permute-done((f32[4,132,2]{2,1,0:T(8,128)S(1)}, f32[4,132,2]{2,1,0:T(8,128)S(1)}, u32[]{:S(2)}, u32[]{:S(2)}) %collective-permute-start.6) | collective-permute-done | bytes 4256 | tf_op jit(solution)/shard_map/ppermute | solution.py:20
  217.1 3.6 collective-permute-done.7
  233.0 4.5 %all-to-all-start.4 = ((f32[8,1,2048]{2,1,0:T(1,128)}), f32[8,1,2048]{2,1,0:T(1,128)S(1)}, u32[]{:S(2)}, u32[]{:S(2)}) async-start(f32[8,1,2048]{2,1,0:T(1,128)} %reshape.939), calls=%async_computation.4 | async-start | bytes 131072 | tf_op jit(solution)/shard_map/all_to_all | solution.py:235
  237.5 4.9 %all-to-all-done.4 = f32[8,1,2048]{2,1,0:T(1,128)S(1)} async-done(((f32[8,1,2048]{2,1,0:T(1,128)}), f32[8,1,2048]{2,1,0:T(1,128)S(1)}, u32[]{:S(2)}, u32[]{:S(2)}) %all-to-all-start.4) | async-done | bytes 65568 | tf_op jit(solution)/shard_map/all_to_all | solution.py:235
  248.7 4.0 all-to-all-start.5
  252.7 4.9 %all-to-all-done.5 = f32[8,1,2048]{2,1,0:T(1,128)S(1)} async-done(((f32[8,1,2048]{2,1,0:T(1,128)}), f32[8,1,2048]{2,1,0:T(1,128)S(1)}, u32[]{:S(2)}, u32[]{:S(2)}) %all-to-all-start.5) | async-done | bytes 65568 | tf_op jit(solution)/shard_map/all_to_all | solution.py:172
  260.8 9.9 %all-to-all-start.6 = ((f32[32,1,512]{2,1,0:T(1,128)}), f32[32,1,512]{2,1,0:T(1,128)S(1)}, u32[]{:S(2)}, u32[]{:S(2)}) async-start(f32[32,1,512]{2,1,0:T(1,128)} %reshape.943), calls=%async_computation.6 | async-start | bytes 131072 | tf_op jit(solution)/shard_map/all_to_all | solution.py:236
  270.7 8.8 %all-to-all-done.6 = f32[32,1,512]{2,1,0:T(1,128)S(1)} async-done(((f32[32,1,512]{2,1,0:T(1,128)}), f32[32,1,512]{2,1,0:T(1,128)S(1)}, u32[]{:S(2)}, u32[]{:S(2)}) %all-to-all-start.6) | async-done | bytes 65568 | tf_op jit(solution)/shard_map/all_to_all | solution.py:236
  280.4 3.0 convolution_bitcast_fusion.7
  288.5 3.0 convolution_bitcast_fusion.6
  299.5 4.8 %reshape.945 = f32[32,1,512]{2,1,0:T(1,128)} reshape(f32[2048,2,4]{2,1,0:T(2,128)} %bitcast.222) | data formatting | bytes 131072
  304.3 4.0 all-to-all-start.7
  311.7 5.5 %all-to-all-done.7 = f32[32,1,512]{2,1,0:T(1,128)S(1)} async-done(((f32[32,1,512]{2,1,0:T(1,128)}), f32[32,1,512]{2,1,0:T(1,128)S(1)}, u32[]{:S(2)}, u32[]{:S(2)}) %all-to-all-start.7) | async-done | bytes 65568 | tf_op jit(solution)/shard_map/all_to_all | solution.py:192
  317.9 4.6 %reshape.946 = f32[2048,2,4]{2,1,0:T(2,128)} reshape(f32[32,512]{1,0:T(8,128)S(1)} %reduce.5) | data formatting | bytes 131072
  325.5 5.2 %collective-permute-start.9 = (f32[4,2,64]{2,1,0:T(2,128)S(1)}, f32[4,2,64]{2,1,0:T(2,128)S(1)}, u32[]{:S(2)}, u32[]{:S(2)}) collective-permute-start(f32[4,2,64]{2,1,0:T(2,128)S(1)} %get-tuple-element.22), channel_id=1, source_target_pairs={{32,0},{64,32},{96,64},{128,96},{160,128},{192,160},{224,192},{33,... | collective-permute-start | bytes 6152 | tf_op jit(solution)/shard_map/ppermute | solution.py:21
  339.6 3.7 collective-permute-done.11
  347.0 4.8 %all-to-all-start.8 = ((f32[8,1,512]{2,1,0:T(1,128)}), f32[8,1,512]{2,1,0:T(1,128)S(1)}, u32[]{:S(2)}, u32[]{:S(2)}) async-start(f32[8,1,512]{2,1,0:T(1,128)} %reshape.947), calls=%async_computation.8 | async-start | bytes 32768 | tf_op jit(solution)/shard_map/all_to_all | solution.py:235
  352.9 3.5 all-to-all-done.8
  365.3 3.9 all-to-all-start.9
  369.7 4.2 %all-to-all-done.9 = f32[8,1,512]{2,1,0:T(1,128)S(1)} async-done(((f32[8,1,512]{2,1,0:T(1,128)}), f32[8,1,512]{2,1,0:T(1,128)S(1)}, u32[]{:S(2)}, u32[]{:S(2)}) %all-to-all-start.9) | async-done | bytes 16416 | tf_op jit(solution)/shard_map/all_to_all | solution.py:172
  376.5 7.5 %all-to-all-start.10 = ((f32[32,1,128]{2,1,0:T(1,128)}), f32[32,1,128]{2,1,0:T(1,128)S(1)}, u32[]{:S(2)}, u32[]{:S(2)}) async-start(f32[32,1,128]{2,1,0:T(1,128)} %reshape.951), calls=%async_computation.10 | async-start | bytes 32768 | tf_op jit(solution)/shard_map/all_to_all | solution.py:236
  384.3 8.0 %all-to-all-done.10 = f32[32,1,128]{2,1,0:T(1,128)S(1)} async-done(((f32[32,1,128]{2,1,0:T(1,128)}), f32[32,1,128]{2,1,0:T(1,128)S(1)}, u32[]{:S(2)}, u32[]{:S(2)}) %all-to-all-start.10) | async-done | bytes 16416 | tf_op jit(solution)/shard_map/all_to_all | solution.py:236
  404.2 3.8 all-to-all-start.11
  408.8 7.8 %all-to-all-done.11 = f32[32,1,128]{2,1,0:T(1,128)S(1)} async-done(((f32[32,1,128]{2,1,0:T(1,128)}), f32[32,1,128]{2,1,0:T(1,128)S(1)}, u32[]{:S(2)}, u32[]{:S(2)}) %all-to-all-start.11) | async-done | bytes 16416 | tf_op jit(solution)/shard_map/all_to_all | solution.py:192
  (781 shorter events, 140.3 us)
Async XLA Ops:
  0.8 8.8 %collective-permute-start.1 = (f32[4,2,256]{2,1,0:T(2,128)S(1)}, f32[4,2,256]{2,1,0:T(2,128)S(1)}, u32[]{:S(2)}, u32[]{:S(2)}) collective-permute-start(f32[4,2,256]{2,1,0:T(2,128)S(1)} %get-tuple-element.10), channel_id=1, source_target_pairs={{32,0},{64,32},{96,64},{128,96},{160,128},{192,160},{224,192},{33,... | collective-permute-start | bytes 24584 | tf_op jit(solution)/shard_map/ppermute | solution.py:21
  5.9 3.7 collective-permute-start
  11.4 4.6 %collective-permute-start.2 = (f32[4,260,2]{1,0,2:T(4,128)S(1)}, f32[4,260,2]{1,0,2:T(4,128)S(1)}, u32[]{:S(2)}, u32[]{:S(2)}) collective-permute-start(f32[4,260,2]{1,0,2:T(4,128)S(1)} %copy.302), channel_id=1, source_target_pairs={{0,1},{1,2},{2,3},{3,4},{4,5},{5,6},{6,7},{7,8},{8,9},{9,10},{10,1... | collective-permute-start | bytes 24968 | tf_op jit(solution)/shard_map/ppermute | solution.py:20
  14.7 4.9 %collective-permute-start.3 = (f32[4,260,2]{1,0,2:T(4,128)S(1)}, f32[4,260,2]{1,0,2:T(4,128)S(1)}, u32[]{:S(2)}, u32[]{:S(2)}) collective-permute-start(f32[4,260,2]{1,0,2:T(4,128)S(1)} %copy.303), channel_id=1, source_target_pairs={{1,0},{2,1},{3,2},{4,3},{5,4},{6,5},{7,6},{8,7},{9,8},{10,9},{11,1... | collective-permute-start | bytes 24968 | tf_op jit(solution)/shard_map/ppermute | solution.py:21
  60.1 12.1 %all-to-all-start = ((f32[4,128,128]{1,0,2:T(4,128)}), f32[4,128,128]{1,0,2:T(4,128)S(1)}, u32[]{:S(2)}, u32[]{:S(2)}) async-start(f32[4,128,128]{1,0,2:T(4,128)} %copy.310), calls=%async_computation | async-start | bytes 524288 | tf_op jit(solution)/shard_map/all_to_all | solution.py:235
  83.3 10.9 %all-to-all-start.1 = ((f32[8,1,8192]{2,1,0:T(1,128)}), f32[8,1,8192]{2,1,0:T(1,128)S(1)}, u32[]{:S(2)}, u32[]{:S(2)}) async-start(f32[8,1,8192]{2,1,0:T(1,128)} %reshape.935), calls=%async_computation.1 | async-start | bytes 524288 | tf_op jit(solution)/shard_map/all_to_all | solution.py:172
  101.4 21.1 %all-to-all-start.2 = ((f32[4,128,128]{2,0,1:T(4,128)}), f32[4,128,128]{2,0,1:T(4,128)S(1)}, u32[]{:S(2)}, u32[]{:S(2)}) async-start(f32[4,128,128]{2,0,1:T(4,128)} %copy.321), calls=%async_computation.2 | async-start | bytes 524288 | tf_op jit(solution)/shard_map/all_to_all | solution.py:236
  161.7 18.2 %all-to-all-start.3 = ((f32[32,1,2048]{2,1,0:T(1,128)}), f32[32,1,2048]{2,1,0:T(1,128)S(1)}, u32[]{:S(2)}, u32[]{:S(2)}) async-start(f32[32,1,2048]{2,1,0:T(1,128)} %reshape.937), calls=%async_computation.3 | async-start | bytes 524288 | tf_op jit(solution)/shard_map/all_to_all | solution.py:192
  200.2 6.7 %collective-permute-start.5 = (f32[4,2,128]{2,1,0:T(2,128)S(1)}, f32[4,2,128]{2,1,0:T(2,128)S(1)}, u32[]{:S(2)}, u32[]{:S(2)}) collective-permute-start(f32[4,2,128]{2,1,0:T(2,128)S(1)} %get-tuple-element.16), channel_id=1, source_target_pairs={{32,0},{64,32},{96,64},{128,96},{160,128},{192,160},{224,192},{33,... | collective-permute-start | bytes 12296 | tf_op jit(solution)/shard_map/ppermute | solution.py:21
  204.2 3.1 collective-permute-start.4
  207.4 9.4 %collective-permute-start.6 = (f32[4,132,2]{2,1,0:T(8,128)S(1)}, f32[4,132,2]{2,1,0:T(8,128)S(1)}, u32[]{:S(2)}, u32[]{:S(2)}) collective-permute-start(f32[4,132,2]{2,1,0:T(8,128)S(1)} %get-tuple-element.12), channel_id=1, source_target_pairs={{0,1},{1,2},{2,3},{3,4},{4,5},{5,6},{6,7},{7,8},{8,9},{9,10},{10,1... | collective-permute-start | bytes 12680 | tf_op jit(solution)/shard_map/ppermute | solution.py:20
  211.0 9.7 %collective-permute-start.7 = (f32[4,132,2]{2,1,0:T(8,128)S(1)}, f32[4,132,2]{2,1,0:T(8,128)S(1)}, u32[]{:S(2)}, u32[]{:S(2)}) collective-permute-start(f32[4,132,2]{2,1,0:T(8,128)S(1)} %get-tuple-element.11), channel_id=1, source_target_pairs={{1,0},{2,1},{3,2},{4,3},{5,4},{6,5},{7,6},{8,7},{9,8},{10,9},{11,1... | collective-permute-start | bytes 12680 | tf_op jit(solution)/shard_map/ppermute | solution.py:21
  233.0 9.4 %all-to-all-start.4 = ((f32[8,1,2048]{2,1,0:T(1,128)}), f32[8,1,2048]{2,1,0:T(1,128)S(1)}, u32[]{:S(2)}, u32[]{:S(2)}) async-start(f32[8,1,2048]{2,1,0:T(1,128)} %reshape.939), calls=%async_computation.4 | async-start | bytes 131072 | tf_op jit(solution)/shard_map/all_to_all | solution.py:235
  248.7 8.9 %all-to-all-start.5 = ((f32[8,1,2048]{2,1,0:T(1,128)}), f32[8,1,2048]{2,1,0:T(1,128)S(1)}, u32[]{:S(2)}, u32[]{:S(2)}) async-start(f32[8,1,2048]{2,1,0:T(1,128)} %reshape.941), calls=%async_computation.5 | async-start | bytes 131072 | tf_op jit(solution)/shard_map/all_to_all | solution.py:172
  259.9 24.1 %copy-start.53 = (f32[16]{0:T(128)S(1)}, f32[16]{0:T(128)}, u32[]{:S(2)}) copy-start(f32[16]{0:T(128)} %constant.708) | copy-start | bytes 196
  259.9 24.4 %copy-start.52 = (f32[8]{0:T(128)S(1)}, f32[8]{0:T(128)}, u32[]{:S(2)}) copy-start(f32[8]{0:T(128)} %constant.714) | copy-start | bytes 100
  259.9 24.7 %copy-start.51 = (f32[4]{0:T(128)S(1)}, f32[4]{0:T(128)}, u32[]{:S(2)}) copy-start(f32[4]{0:T(128)} %constant.720) | copy-start | bytes 52
  259.9 27.1 %copy-start.50 = (f32[7]{0:T(128)S(1)}, f32[7]{0:T(128)}, u32[]{:S(2)}) copy-start(f32[7]{0:T(128)} %constant.712) | copy-start | bytes 88
  259.9 27.5 %copy-start.49 = (f32[15]{0:T(128)S(1)}, f32[15]{0:T(128)}, u32[]{:S(2)}) copy-start(f32[15]{0:T(128)} %constant.706) | copy-start | bytes 184
  260.0 28.5 %copy-start.85 = (f32[32,64]{1,0:T(8,128)S(1)}, f32[32,64]{1,0:T(8,128)}, u32[]{:S(2)}) copy-start(f32[32,64]{1,0:T(8,128)} %constant.348.clone) | copy-start | bytes 24580
  260.8 18.7 %all-to-all-start.6 = ((f32[32,1,512]{2,1,0:T(1,128)}), f32[32,1,512]{2,1,0:T(1,128)S(1)}, u32[]{:S(2)}, u32[]{:S(2)}) async-start(f32[32,1,512]{2,1,0:T(1,128)} %reshape.943), calls=%async_computation.6 | async-start | bytes 131072 | tf_op jit(solution)/shard_map/all_to_all | solution.py:236
  304.3 12.9 %all-to-all-start.7 = ((f32[32,1,512]{2,1,0:T(1,128)}), f32[32,1,512]{2,1,0:T(1,128)S(1)}, u32[]{:S(2)}, u32[]{:S(2)}) async-start(f32[32,1,512]{2,1,0:T(1,128)} %reshape.945), calls=%async_computation.7 | async-start | bytes 131072 | tf_op jit(solution)/shard_map/all_to_all | solution.py:192
  322.5 20.8 %copy-start.34 = (f32[65]{0:T(128)S(1)}, f32[65]{0:T(128)}, u32[]{:S(2)}) copy-start(f32[65]{0:T(128)} %get-tuple-element.101) | copy-start | bytes 784
  322.5 20.8 %copy-start.35 = (f32[65]{0:T(128)S(1)}, f32[65]{0:T(128)}, u32[]{:S(2)}) copy-start(f32[65]{0:T(128)} %get-tuple-element.102) | copy-start | bytes 784
  325.5 7.4 %collective-permute-start.9 = (f32[4,2,64]{2,1,0:T(2,128)S(1)}, f32[4,2,64]{2,1,0:T(2,128)S(1)}, u32[]{:S(2)}, u32[]{:S(2)}) collective-permute-start(f32[4,2,64]{2,1,0:T(2,128)S(1)} %get-tuple-element.22), channel_id=1, source_target_pairs={{32,0},{64,32},{96,64},{128,96},{160,128},{192,160},{224,192},{33,... | collective-permute-start | bytes 6152 | tf_op jit(solution)/shard_map/ppermute | solution.py:21
  330.7 3.1 collective-permute-start.8
  333.9 5.6 %collective-permute-start.10 = (f32[4,68,2]{2,1,0:T(8,128)S(1)}, f32[4,68,2]{2,1,0:T(8,128)S(1)}, u32[]{:S(2)}, u32[]{:S(2)}) collective-permute-start(f32[4,68,2]{2,1,0:T(8,128)S(1)} %get-tuple-element.17), channel_id=1, source_target_pairs={{0,1},{1,2},{2,3},{3,4},{4,5},{5,6},{6,7},{7,8},{8,9},{9,10},{10,1... | collective-permute-start | bytes 6536 | tf_op jit(solution)/shard_map/ppermute | solution.py:20
  336.4 6.9 %collective-permute-start.11 = (f32[4,68,2]{2,1,0:T(8,128)S(1)}, f32[4,68,2]{2,1,0:T(8,128)S(1)}, u32[]{:S(2)}, u32[]{:S(2)}) collective-permute-start(f32[4,68,2]{2,1,0:T(8,128)S(1)} %get-tuple-element.18), channel_id=1, source_target_pairs={{1,0},{2,1},{3,2},{4,3},{5,4},{6,5},{7,6},{8,7},{9,8},{10,9},{11,1... | collective-permute-start | bytes 6536 | tf_op jit(solution)/shard_map/ppermute | solution.py:21
  347.0 9.4 %all-to-all-start.8 = ((f32[8,1,512]{2,1,0:T(1,128)}), f32[8,1,512]{2,1,0:T(1,128)S(1)}, u32[]{:S(2)}, u32[]{:S(2)}) async-start(f32[8,1,512]{2,1,0:T(1,128)} %reshape.947), calls=%async_computation.8 | async-start | bytes 32768 | tf_op jit(solution)/shard_map/all_to_all | solution.py:235
  365.3 8.6 %all-to-all-start.9 = ((f32[8,1,512]{2,1,0:T(1,128)}), f32[8,1,512]{2,1,0:T(1,128)S(1)}, u32[]{:S(2)}, u32[]{:S(2)}) async-start(f32[8,1,512]{2,1,0:T(1,128)} %reshape.949), calls=%async_computation.9 | async-start | bytes 32768 | tf_op jit(solution)/shard_map/all_to_all | solution.py:172
  369.5 23.6 %copy-start.4 = (f32[32,32,32]{2,1,0:T(8,128)S(1)}, f32[32,32,32]{2,1,0:T(8,128)}, u32[]{:S(2)}) copy-start(f32[32,32,32]{2,1,0:T(8,128)} %constant.355.clone) | copy-start | bytes 393220
  374.5 20.7 %copy-start.79 = (f32[4]{0:T(128)S(1)}, f32[4]{0:T(128)}, u32[]{:S(2)}) copy-start(f32[4]{0:T(128)} %constant.812) | copy-start | bytes 52
  374.5 20.8 %copy-start.78 = (f32[2]{0:T(128)S(1)}, f32[2]{0:T(128)}, u32[]{:S(2)}) copy-start(f32[2]{0:T(128)} %constant.818) | copy-start | bytes 28
  374.5 21.4 %copy-start.77 = (f32[3]{0:T(128)S(1)}, f32[3]{0:T(128)}, u32[]{:S(2)}) copy-start(f32[3]{0:T(128)} %constant.810) | copy-start | bytes 40
  374.5 21.7 %copy-start.76 = (f32[7]{0:T(128)S(1)}, f32[7]{0:T(128)}, u32[]{:S(2)}) copy-start(f32[7]{0:T(128)} %constant.804) | copy-start | bytes 88
  374.6 21.9 %copy-start.75 = (f32[15]{0:T(128)S(1)}, f32[15]{0:T(128)}, u32[]{:S(2)}) copy-start(f32[15]{0:T(128)} %constant.798) | copy-start | bytes 184
  375.3 21.6 %copy-start.5 = (f32[32,32,32]{2,1,0:T(8,128)S(1)}, f32[32,32,32]{2,1,0:T(8,128)}, u32[]{:S(2)}) copy-start(f32[32,32,32]{2,1,0:T(8,128)} %constant.357.clone) | copy-start | bytes 393220
  375.3 21.6 %copy-start.19 = (f32[32,32]{1,0:T(8,128)S(1)}, f32[32,32]{1,0:T(8,128)}, u32[]{:S(2)}) copy-start(f32[32,32]{1,0:T(8,128)} %constant.356.clone) | copy-start | bytes 12292
  375.6 22.9 %copy-start.74 = (f32[16]{0:T(128)S(1)}, f32[16]{0:T(128)}, u32[]{:S(2)}) copy-start(f32[16]{0:T(128)} %constant.830) | copy-start | bytes 196
  375.6 23.2 %copy-start.73 = (f32[8]{0:T(128)S(1)}, f32[8]{0:T(128)}, u32[]{:S(2)}) copy-start(f32[8]{0:T(128)} %constant.837) | copy-start | bytes 100
  375.6 23.5 %copy-start.72 = (f32[4]{0:T(128)S(1)}, f32[4]{0:T(128)}, u32[]{:S(2)}) copy-start(f32[4]{0:T(128)} %constant.843) | copy-start | bytes 52
  375.6 23.7 %copy-start.71 = (f32[2]{0:T(128)S(1)}, f32[2]{0:T(128)}, u32[]{:S(2)}) copy-start(f32[2]{0:T(128)} %constant.849) | copy-start | bytes 28
  375.6 24.4 %copy-start.70 = (f32[3]{0:T(128)S(1)}, f32[3]{0:T(128)}, u32[]{:S(2)}) copy-start(f32[3]{0:T(128)} %constant.841) | copy-start | bytes 40
  375.6 24.7 %copy-start.69 = (f32[7]{0:T(128)S(1)}, f32[7]{0:T(128)}, u32[]{:S(2)}) copy-start(f32[7]{0:T(128)} %constant.835) | copy-start | bytes 88
  375.7 25.0 %copy-start.68 = (f32[15]{0:T(128)S(1)}, f32[15]{0:T(128)}, u32[]{:S(2)}) copy-start(f32[15]{0:T(128)} %constant.827) | copy-start | bytes 184
  375.7 25.3 %copy-start.18 = (f32[32,32]{1,0:T(8,128)S(1)}, f32[32,32]{1,0:T(8,128)}, u32[]{:S(2)}) copy-start(f32[32,32]{1,0:T(8,128)} %constant.358.clone) | copy-start | bytes 12292
  376.5 15.9 %all-to-all-start.10 = ((f32[32,1,128]{2,1,0:T(1,128)}), f32[32,1,128]{2,1,0:T(1,128)S(1)}, u32[]{:S(2)}, u32[]{:S(2)}) async-start(f32[32,1,128]{2,1,0:T(1,128)} %reshape.951), calls=%async_computation.10 | async-start | bytes 32768 | tf_op jit(solution)/shard_map/all_to_all | solution.py:236
  404.2 12.4 %all-to-all-start.11 = ((f32[32,1,128]{2,1,0:T(1,128)}), f32[32,1,128]{2,1,0:T(1,128)S(1)}, u32[]{:S(2)}, u32[]{:S(2)}) async-start(f32[32,1,128]{2,1,0:T(1,128)} %reshape.953), calls=%async_computation.11 | async-start | bytes 32768 | tf_op jit(solution)/shard_map/all_to_all | solution.py:192
  (63 other events, 646.7 us)
where the time goes:
time: 429 us; the launch traced here: 422 us
  local copies, waits for them, and re-layouts  171 us (40%)
  starting transfers between devices  104 us (24%)
  waiting for transfers between devices  85.9 us (20%)
  other arithmetic  33.4 us (8%)
  matrix products  24.3 us (6%)
    unnamed x215, local copies, waits for them, and re-layouts  55.8 us
    all_to_all x3, starting transfers between devices, shards(): lax.all_to_all(across, 'gy', split_axis=1, concat_axis=2, tiled=True)  28.9 us
    all_to_all x3, waiting for transfers between devices, shards(): lax.all_to_all(across, 'gy', split_axis=1, concat_axis=2, tiled=True)  25.1 us
    ppermute x6, starting transfers between devices, padded_2(): after = lax.ppermute(initial, axis, down)  18.2 us
    all_to_all x3, waiting for transfers between devices, full_rows(): return lax.all_to_all(solved, 'gx', split_axis=1, concat_axis=2, tiled=True)  15.6 us
    ppermute x6, starting transfers between devices, padded_2(): before = lax.ppermute(last, axis, up)  15.2 us
    all_to_all x3, starting transfers between devices, shards(): lax.all_to_all(scaled, 'gx', split_axis=2, concat_axis=1, tiled=True)  14.9 us
    all_to_all x3, starting transfers between devices, full_cols(): return lax.all_to_all(solved, 'gy', split_axis=2, concat_axis=1, tiled=True)  14.1 us
  transfers between devices with their start and end apart: 24, of which 18 were waited for; matrix products, arithmetic and copies ran while one was open for 6% of the time, Pallas kernels for 0%

commit v1 on v0

v1 whole, which is shorter than its diff:
```python
import functools

import jax
import jax.numpy as jnp
import numpy as np
from jax import lax
from jax.experimental import pallas as pl
from jax.experimental.pallas import tpu as pltpu
from jax.sharding import PartitionSpec as P

LEVELS = 3
DEPTH = 4
LENGTH = 64.0
MESH = pl.DeviceIdType.MESH
TABLE_LANES = 384


def padded_rows(count):
    return count + 8


def padded_lanes(count):
    return (count // 128 + 1) * 128 if count >= 128 else 128


def solver_line(count):
    off = 1.0 / (3.0 * LENGTH) - LENGTH
    inner = 4.0 / (3.0 * LENGTH) + 2.0 * LENGTH
    end = 2.0 / (3.0 * LENGTH) + LENGTH
    diag = np.full(count, inner)
    diag[0] = diag[-1] = end
    q = np.ones(count)
    p = np.ones(count)
    q[1] = -diag[0] / off
    p[-2] = -diag[-1] / off
    for i in range(1, count - 1):
        q[i + 1] = -(diag[i] * q[i]) / off - q[i - 1]
        j = count - 1 - i
        p[j - 1] = -(diag[j] * p[j]) / off - p[j + 1]
    return q, p, diag[0] * p[0] + off * p[1]


def load_block(total, coarse_ids, fine_ids):
    out = np.zeros((len(coarse_ids), len(fine_ids)))

    def mass(i, j):
        if i < 0 or i >= total or j < 0 or j >= total:
            return 0.0
        if i == j:
            return (2.0 if i in (0, total - 1) else 4.0) / 6.0
        return 1.0 / 6.0 if abs(i - j) == 1 else 0.0

    for a, k in enumerate(coarse_ids):
        if k < 0 or k >= total // 2:
            continue
        upper = 1.0 if 2 * k + 1 == total - 1 else 0.5
        for b in range(max(0, 2 * k - 2 - fine_ids[0]), min(len(fine_ids), 2 * k + 3 - fine_ids[0])):
            j = fine_ids[b]
            out[a, b] = mass(2 * k, j) + 0.5 * mass(2 * k - 1, j) + upper * mass(2 * k + 1, j)
    return out


def line_tables(total, tiles):
    n = total // tiles
    h = n // 2
    coarse = total // 2
    q, p, w = solver_line(coarse)
    local, functional, carry, weight, select = [], [], [], [], []
    for t in range(tiles):
        first = t * h
        last_tile = t == tiles - 1
        ids = np.arange(first, first + h + 1)
        if last_tile:
            ids[h] = ids[h - 2]
        window = np.arange(first - 1, first + h + 2)
        load = load_block(total, window, np.arange(t * n, t * n + n + 1))
        inside = (window >= 0) & (window < coarse)
        safe = np.clip(window, 0, coarse - 1)
        low = np.minimum(ids[:, None], safe[None, :])
        high = np.maximum(ids[:, None], safe[None, :])
        green = np.where(inside[None, :], q[low] * p[high] / w, 0.0)
        local.append(green @ load)
        q_end = q[min(first + h, coarse - 1)]
        to_right = (np.where(inside, q[safe] / q_end, 0.0)) @ load
        to_left = (np.where(inside, p[safe] / p[first], 0.0)) @ load
        to_right[n] = 0.0
        to_left[0] = 0.0
        functional.append(np.stack([to_right, to_left]))
        carry.append(np.stack([p[ids] / p[first], q[ids] / q_end]))
        weights = np.zeros((2, tiles))
        for k in range(1, tiles):
            s = (t - k) % tiles
            if s < t:
                weights[0, k] = q[(s + 1) * h] * p[first] / w
            else:
                weights[1, k] = q_end * p[s * h] / w
        weight.append(weights)
        pick = np.zeros((n + 1, h + 1))
        pick[2 * np.arange(h), np.arange(h)] = 1.0
        pick[n - 4 if last_tile else n, h] = 1.0
        select.append(pick)
    return [np.stack(item) for item in (local, functional, carry, weight, select)]


def fit(array, shape):
    out = np.zeros(array.shape[: array.ndim - len(shape)] + tuple(shape))
    out[tuple(slice(0, size) for size in array.shape)] = array
    return out


@functools.lru_cache(maxsize=None)
def tables(nx, ny, gx, gy):
    row_mats, col_mats, selects = [], [], []
    row_vecs = np.zeros((gx, LEVELS, 8, TABLE_LANES))
    col_vecs = np.zeros((gy, LEVELS, 8, TABLE_LANES))
    row_w = np.zeros((gx, LEVELS, 2, gx))
    col_w = np.zeros((gy, LEVELS, 2, gy))
    for level in range(LEVELS):
        for vecs, ws, total, tiles in ((row_vecs, row_w, nx >> level, gx), (col_vecs, col_w, ny >> level, gy)):
            n = total // tiles
            h = n // 2
            local, functional, carry, weight, select = line_tables(total, tiles)
            vecs[:, level, 0:2, : n + 1] = functional
            vecs[:, level, 2:4, : h + 1] = carry
            ws[:, level] = weight
            if vecs is row_vecs:
                row_mats.append(fit(local, (padded_rows(h), padded_rows(n))))
            else:
                joined = np.concatenate([local, functional], axis=1).transpose(0, 2, 1)
                shape = (padded_lanes(n), padded_lanes(h))
                col_mats.append(fit(joined, shape))
                selects.append(fit(select[[0, -1]], shape))
    as32 = lambda item: np.ascontiguousarray(item, np.float32)
    return (
        [as32(m) for m in row_mats],
        [as32(m) for m in col_mats],
        [as32(m) for m in selects],
        as32(row_vecs),
        as32(col_vecs),
        as32(row_w.reshape(-1)),
        as32(col_w.reshape(-1)),
    )


def dot(a, b, dims=((1,), (0,))):
    return lax.dot_general(
        a, b, (dims, ((), ())), precision=lax.Precision.HIGHEST, preferred_element_type=jnp.float32
    )


def iota(shape, dim):
    return lax.broadcasted_iota(jnp.int32, shape, dim)


def detail(u):
    rows, lanes = u.shape
    odd_lane = iota(u.shape, 1) % 2 == 1
    odd_row = iota(u.shape, 0) % 2 == 1
    along = jnp.where(odd_lane, 0.5 * (pltpu.roll(u, 1, 1) + pltpu.roll(u, lanes - 1, 1)), u)
    both = jnp.where(odd_row, 0.5 * (pltpu.roll(along, 1, 0) + pltpu.roll(along, rows - 1, 0)), along)
    return u - both


def spread_matrix(count, lanes, stride, width):
    shape = (lanes, width)
    row = iota(shape, 0)
    return jnp.where((iota(shape, 1) == stride * row) & (row < count), 1.0, 0.0).astype(jnp.float32)


def kernel(gx_n, gy_n, n0, *refs):
    (sal, rm0, rm1, rm2, cm0, cm1, cm2, se0, se1, se2, row_vecs, col_vecs, row_w, col_w, out) = refs[:15]
    (u0, u1, u2, w0, w1, w2, out_v, tall_v, rmv0, rmv1, rmv2, cmv0, cmv1, cmv2, sev0, sev1, sev2, rv, cv,
     hrow, hcol, hcorner, hrow_in, hcol_in, hcorner_in,
     xs0, xs1, xs2, xr0, xr1, xr2, ys0, ys1, ys2, yr0, yr1, yr2,
     load_sem, halo_send, halo_recv, x_send, x_recv, y_send, y_recv, out_sem) = refs[15:]
    us, ws = (u0, u1, u2), (w0, w1, w2)
    row_mats, col_mats, selects = (rmv0, rmv1, rmv2), (cmv0, cmv1, cmv2), (sev0, sev1, sev2)
    xs, xr, ys, yr = (xs0, xs1, xs2), (xr0, xr1, xr2), (ys0, ys1, ys2), (yr0, yr1, yr2)
    gx, gy = lax.axis_index("gx"), lax.axis_index("gy")
    last_x, last_y = gx == gx_n - 1, gy == gy_n - 1
    is_last_col = (gy + 1) // gy_n

    loads = [pltpu.make_async_copy(sal, u0.at[:, pl.ds(0, n0), pl.ds(0, n0)], load_sem.at[0])]
    later = [(rv, row_vecs.at[gx]), (cv, col_vecs.at[gy])]
    for src, dst in zip((rm0, rm1, rm2), row_mats):
        later.append((dst, src.at[gx]))
    for src, dst in zip((cm0, cm1, cm2), col_mats):
        later.append((dst, src.at[gy]))
    for src, dst in zip((se0, se1, se2), selects):
        later.append((dst, src.at[is_last_col]))
    for i, (dst, src) in enumerate(later):
        loads.append(pltpu.make_async_copy(src, dst, load_sem.at[1 + i]))
    for copy in loads:
        copy.start()

    barrier = pltpu.get_barrier_semaphore()
    x_peers = [(lax.rem(gx + k, gx_n), gy) for k in range(1, gx_n)]
    y_peers = [(gx, lax.rem(gy + k, gy_n)) for k in range(1, gy_n)]
    up, left = lax.rem(gx + gx_n - 1, gx_n), lax.rem(gy + gy_n - 1, gy_n)
    greeted = x_peers + y_peers + [(lax.rem(gx + 1, gx_n), lax.rem(gy + 1, gy_n))]
    for peer in greeted:
        pl.semaphore_signal(barrier, inc=1, device_id=peer, device_id_type=MESH)

    loads[0].wait()
    edge = jnp.where(iota((DEPTH, n0), 1) == 0, 1.0, 0.0)
    depth_row = iota((DEPTH, n0), 0)
    hrow[...] = u0[:, 0, 0:n0]
    hcorner[...] = u0[:, 0, 0:128]
    first_cols = jnp.zeros((DEPTH, n0), jnp.float32)
    for d in range(DEPTH):
        first_cols += dot(jnp.where(depth_row == d, edge, 0.0), u0[d, 0:n0, 0:n0], ((1,), (1,)))
    hcol[...] = first_cols
    pl.semaphore_wait(barrier, len(greeted))
    halos = []
    for i, (src, dst, peer) in enumerate(
        ((hrow, hrow_in, (up, gy)), (hcol, hcol_in, (gx, left)), (hcorner, hcorner_in, (up, left)))
    ):
        copy = pltpu.make_async_remote_copy(
            src_ref=src, dst_ref=dst, send_sem=halo_send.at[i], recv_sem=halo_recv.at[i],
            device_id=peer, device_id_type=MESH,
        )
        copy.start()
        halos.append(copy)
    for copy in loads[1:]:
        copy.wait()
    for copy in halos:
        copy.wait_recv()
    lane0 = iota((n0, 128), 1) == 0
    first_row = iota((8, 1), 0) == 0
    cols_in = jnp.concatenate([hcol_in[...], jnp.zeros((4, n0), jnp.float32)], axis=0).T
    for d in range(DEPTH):
        own_alias = u0[d, 0:n0, n0 - 2 : n0 - 1]
        column = jnp.where(last_y, own_alias, cols_in[:, d : d + 1])
        u0[d, 0:n0, n0 : n0 + 128] = jnp.where(lane0, column, 0.0)
        row = jnp.where(last_x, u0[d, n0 - 2 : n0 - 1, 0:n0], hrow_in[d : d + 1, :])
        corner = jnp.where(
            last_y,
            row[:, n0 - 2 : n0 - 1],
            jnp.where(last_x, u0[d, n0 - 2 : n0 - 1, n0 : n0 + 1], hcorner_in[d : d + 1, 0:1]),
        )
        u0[d, n0 : n0 + 8, 0:n0] = jnp.where(first_row, row, 0.0)
        u0[d, n0 : n0 + 8, n0 : n0 + 128] = jnp.where(first_row & (iota((8, 128), 1) == 0), corner, 0.0)

    def send_all(peers, me, count, src, dst, send, recv):
        for k, peer in enumerate(peers):
            pltpu.make_async_remote_copy(
                src_ref=src.at[(me + k + 1) // count], dst_ref=dst.at[k], send_sem=send, recv_sem=recv,
                device_id=peer, device_id_type=MESH,
            ).start()

    def gather(buf, weights, base, count):
        right = jnp.zeros(buf.shape[1:], jnp.float32)
        left_sum = jnp.zeros(buf.shape[1:], jnp.float32)
        for k in range(1, count):
            part = buf[k - 1]
            right += weights[base + k] * part
            left_sum += weights[base + count + k] * part
        return right, left_sum

    for level in range(LEVELS):
        n = n0 >> level
        h = n // 2
        rows, lanes = padded_rows(n), padded_lanes(n)
        rows_c, lanes_c = padded_rows(h), padded_lanes(h)
        tall = padded_lanes(h)
        u, w = us[level], ws[level]
        col_mat, row_mat, select = col_mats[level][...], row_mats[level][...], selects[level][...]
        q_cols = rv[level, :, 0:rows if rows % 128 == 0 else padded_lanes(n)].T
        right_rows, left_rows = [], []
        for d in range(DEPTH):
            value = detail(u[d])
            w[d] = value
            right_rows.append(jnp.sum(value * q_cols[0:rows, 0:1], axis=0, keepdims=True))
            left_rows.append(jnp.sum(value * q_cols[0:rows, 1:2], axis=0, keepdims=True))
        xs[level][0] = jnp.concatenate(right_rows, axis=0)
        xs[level][1] = jnp.concatenate(left_rows, axis=0)
        send_all(x_peers, gx, gx_n, xs[level], xr[level], x_send.at[level], x_recv.at[level])

        base, cols_local = [], jnp.zeros((8, rows_c), jnp.float32)
        row8 = iota((8, lanes_c), 0)
        lane8 = iota((8, lanes_c), 1)
        is_tail = iota((rows_c, lanes_c), 0) == h
        for d in range(DEPTH):
            z = dot(row_mat, dot(w[d], col_mat))
            pick = ((row8 == d) & (lane8 == h + 1)) | ((row8 == 4 + d) & (lane8 == h + 2))
            cols_local += dot(jnp.where(pick, 1.0, 0.0), z, ((1,), (1,)))
            even = even_rows(tall_v, dot(u[d], select), rows_c)
            even = jnp.where(is_tail & last_x, even[h - 2 : h - 1, :], even)
            base.append(jnp.where(iota((rows_c, lanes_c), 1) <= h, z, 0.0) + even)
        if rows_c < tall:
            cols_local = jnp.concatenate([cols_local, jnp.zeros((8, tall - rows_c), jnp.float32)], axis=1)

        if level == 0:
            for d in range(DEPTH):
                for j in range(out_v.shape[1]):
                    out_v[d, j] = w0[d, 0:n0, 128 * j : 128 * j + 128]
        else:
            mat = spread_matrix(n, lanes, 1 << level, n0)
            for d in range(DEPTH):
                add_rows(out_v, d, dot(w[d, 0:n, :], mat), 1 << level)

        pltpu.make_async_copy(xr[level], xr[level], x_recv.at[level]).wait()
        a_right, a_left = gather(xr[level], row_w, (gx * LEVELS + level) * 2 * gx_n, gx_n)
        q_r, q_l = cv[level, 0:1, 0:lanes], cv[level, 1:2, 0:lanes]
        p_r, p_l = rv[level, 2:3, 0:tall], rv[level, 3:4, 0:tall]

        def line(value, functional):
            return jnp.sum(value * functional, axis=1, keepdims=True)

        ys[level][0] = cols_local[0:4] + line(a_right, q_r) * p_r + line(a_left, q_r) * p_l
        ys[level][1] = cols_local[4:8] + line(a_right, q_l) * p_r + line(a_left, q_l) * p_l
        send_all(y_peers, gy, gy_n, ys[level], yr[level], y_send.at[level], y_recv.at[level])

        carried = dot(jnp.concatenate([a_right, a_left], axis=0), col_mat)
        carried = jnp.where(iota((8, lanes_c), 1) <= h, carried, 0.0)
        py_r, py_l = cv[level, 2:3, 0:lanes_c], cv[level, 3:4, 0:lanes_c]
        shapes = jnp.concatenate([jnp.broadcast_to(py_r, (4, lanes_c)), jnp.broadcast_to(py_l, (4, lanes_c))], axis=0)
        own = jnp.concatenate([jnp.broadcast_to(p_r, (4, tall)), jnp.broadcast_to(p_l, (4, tall))], axis=0)
        other = jnp.concatenate([carried, shapes], axis=0)

        pltpu.make_async_copy(yr[level], yr[level], y_recv.at[level]).wait()
        c_right, c_left = gather(yr[level], col_w, (gy * LEVELS + level) * 2 * gy_n, gy_n)
        lhs = jnp.concatenate([own, c_right, c_left], axis=0).T[0:rows_c]
        for d in range(DEPTH):
            chosen = jnp.where(iota((16, lanes_c), 0) % 4 == d, other, 0.0)
            new = base[d] + dot(lhs, chosen)
            if level + 1 < LEVELS:
                us[level + 1][d] = new
            else:
                mat = spread_matrix(h, lanes_c, 2 << level, n0)
                add_rows(out_v, d, dot(new[0:h], mat), 2 << level)

    results = []
    for j in range(out_v.shape[1]):
        results.append(pltpu.make_async_copy(out_v.at[:, j], out.at[:, :, pl.ds(128 * j, 128)], out_sem.at[j]))
        results[-1].start()
    for i, copy in enumerate(halos):
        copy.wait_send()
    for level in range(LEVELS):
        pltpu.make_async_copy(xr[level], xr[level], x_send.at[level]).wait()
        pltpu.make_async_copy(yr[level], yr[level], y_send.at[level]).wait()
    for copy in results:
        copy.wait()


def even_rows(tall_v, value, rows_c):
    rows, lanes = value.shape
    half = rows // 2
    parts = []
    for j in range(lanes // 128):
        tall_v[j, 0:rows] = value[:, 128 * j : 128 * j + 128]
        part = tall_v[j, pl.ds(0, half, stride=2), :]
        parts.append(jnp.concatenate([part, jnp.zeros((rows_c - half, 128), jnp.float32)], axis=0))
    return jnp.concatenate(parts, axis=1)


def add_rows(ref, d, value, stride):
    place = pl.ds(0, value.shape[0], stride=stride)
    for j in range(ref.shape[1]):
        ref[d, j, place, :] = ref[d, j, place, :] + value[:, 128 * j : 128 * j + 128]


def shards(salinity):
    gx_n, gy_n = lax.axis_size("gx"), lax.axis_size("gy")
    _, nx, ny = salinity.shape
    n0 = nx
    row_mats, col_mats, selects, row_vecs, col_vecs, row_w, col_w = tables(nx * gx_n, ny * gy_n, gx_n, gy_n)
    scratch = []
    vmem = lambda *shape: pltpu.VMEM(shape, jnp.float32)
    sizes = [n0 >> level for level in range(LEVELS)]
    scratch += [vmem(DEPTH, padded_rows(n), padded_lanes(n)) for n in sizes]
    scratch += [vmem(DEPTH, padded_rows(n), padded_lanes(n)) for n in sizes]
    scratch += [vmem(DEPTH, n0 // 128, n0, 128), vmem(2, padded_rows(n0), 128)]
    for group in (row_mats, col_mats, selects):
        scratch += [vmem(*m.shape[1:]) for m in group]
    scratch += [vmem(*row_vecs.shape[1:]), vmem(*col_vecs.shape[1:])]
    scratch += [vmem(DEPTH, n0), vmem(DEPTH, n0), vmem(DEPTH, 128)] * 2
    scratch += [vmem(2, DEPTH, padded_lanes(n)) for n in sizes]
    scratch += [vmem(gx_n - 1, DEPTH, padded_lanes(n)) for n in sizes]
    scratch += [vmem(2, DEPTH, padded_lanes(n // 2)) for n in sizes]
    scratch += [vmem(gy_n - 1, DEPTH, padded_lanes(n // 2)) for n in sizes]
    scratch += [pltpu.SemaphoreType.DMA((12,)), pltpu.SemaphoreType.DMA((3,)), pltpu.SemaphoreType.DMA((3,))]
    scratch += [pltpu.SemaphoreType.DMA((LEVELS,))] * 4
    scratch += [pltpu.SemaphoreType.DMA((n0 // 128,))]
    anywhere = pl.BlockSpec(memory_space=pl.ANY)
    scalars = pl.BlockSpec(memory_space=pltpu.SMEM)
    return pl.pallas_call(
        functools.partial(kernel, gx_n, gy_n, n0),
        out_shape=jax.ShapeDtypeStruct(salinity.shape, jnp.float32),
        in_specs=[anywhere] * 12 + [scalars] * 2,
        out_specs=anywhere,
        scratch_shapes=scratch,
        compiler_params=pltpu.CompilerParams(
            collective_id=0, has_side_effects=True, vmem_limit_bytes=48 * 1024 * 1024
        ),
    )(salinity, *row_mats, *col_mats, *selects, row_vecs, col_vecs, row_w, col_w)


def solution(mesh):
    placed = P(None, "gx", "gy")
    return jax.shard_map(shards, mesh=mesh, in_specs=(placed,), out_specs=placed, check_vma=False)
```

time: 429 us -> 65 us (0.15); the launches traced: 422 us -> 64.6 us
  local copies, waits for them, and re-layouts: 171 us -> 10.8 us
  starting transfers between devices: 104 us -> 0 us
  waiting for transfers between devices: 85.9 us -> 0 us
  Pallas kernels: 0 us -> 53.8 us
  other arithmetic: 33.4 us -> 0 us
  matrix products: 24.3 us -> 0 us
    slice x199 -> x0, local copies, waits for them, and re-layouts: 75.4 us -> none  [the longest x6 13.9 us: restrict(): upper = lax.slice_in_dim(mass, 2, count + 1, 2, axis=axis)]
    all_to_all x12 -> x0, starting transfers between devices: 70.2 us -> none  [the longest x3 28.9 us: shards(): lax.all_to_all(across, 'gy', split_axis=1, concat_axis=2, tiled=True)]
    all_to_all x12 -> x0, waiting for transfers between devices: 67.7 us -> none  [the longest x3 25.1 us: shards(): lax.all_to_all(across, 'gy', split_axis=1, concat_axis=2, tiled=True)]
    pallas_call x0 -> x1, Pallas kernels: none -> 53.8 us  [shards(): pl.pallas_call(functools.partial(kernel, gx_n, gy_n, n0), out_shape=jax.S...]
    unnamed x215 -> x21, local copies, waits for them, and re-layouts: 55.8 us -> 10.8 us
    ppermute x12 -> x0, starting transfers between devices: 33.4 us -> none  [the longest x6 18.2 us: padded_2(): after = lax.ppermute(initial, axis, down)]
    dot_general x15 -> x0, matrix products: 24.3 us -> none  [the longest x3 9.14 us: full_cols(): jnp.einsum('sik,dask->dasi', b_tab, forward, precision=lax.Precision.HIGH...]
    ppermute x12 -> x0, waiting for transfers between devices: 18.3 us -> none  [the longest x6 10.7 us: padded_2(): after = lax.ppermute(initial, axis, down)]
  transfers between devices with their start and end apart: 24 -> 0, of which waited for: 18 -> 0; matrix products, arithmetic and copies ran while one was open for 6% -> 0% of each run, Pallas kernels for 0% -> 0%
where the time goes in v1:
time: 65 us; the launch traced here: 64.6 us
  Pallas kernels  53.8 us (83%)
  local copies, waits for them, and re-layouts  10.8 us (17%)
    pallas_call x1, Pallas kernels, shards(): pl.pallas_call(functools.partial(kernel, gx_n, gy_n, n0), out_shape=jax.S...  53.8 us
    unnamed x21, local copies, waits for them, and re-layouts  10.8 us

profile of v1, /device:TPU:1, one launch (start us, length us, event | category | flops | bytes accessed | tf_op | source)
XLA Modules:
  0.0 64.6 jit_solution(6067151732799319600)
XLA Ops:
  0.0 0.0 copy-start
  0.0 1.3 %copy-done = f32[32,3,8,384]{3,2,1,0:T(8,128)S(1)} copy-done((f32[32,3,8,384]{3,2,1,0:T(8,128)S(1)}, f32[32,3,8,384]{3,2,1,0:T(8,128)}, u32[]{:S(2)}) %copy-start) | copy-done | bytes 1179672
  1.3 0.0 copy-start.1
  1.3 1.2 %copy-done.1 = f32[4,256,256]{2,1,0:T(8,128)S(1)} copy-done((f32[4,256,256]{2,1,0:T(8,128)S(1)}, f32[4,256,256]{2,1,0:T(8,128)}, u32[]{:S(2)}) %copy-start.1) | copy-done | bytes 1048600
  2.5 0.0 copy-start.2
  2.5 1.1 %copy-done.2 = f32[2,384,256]{2,1,0:T(8,128)S(1)} copy-done((f32[2,384,256]{2,1,0:T(8,128)S(1)}, f32[2,384,256]{2,1,0:T(8,128)}, u32[]{:S(2)}) %copy-start.2) | copy-done | bytes 786456
  3.6 0.0 copy-start.3
  3.6 1.1 %copy-done.3 = f32[8,72,136]{2,1,0:T(8,128)S(1)} copy-done((f32[8,72,136]{2,1,0:T(8,128)S(1)}, f32[8,72,136]{2,1,0:T(8,128)}, u32[]{:S(2)}) %copy-start.3) | copy-done | bytes 313368
  4.7 0.0 copy-start.4
  4.7 1.0 %copy-done.4 = f32[8,3,8,384]{3,2,1,0:T(8,128)S(1)} copy-done((f32[8,3,8,384]{3,2,1,0:T(8,128)S(1)}, f32[8,3,8,384]{3,2,1,0:T(8,128)}, u32[]{:S(2)}) %copy-start.4) | copy-done | bytes 294936
  5.7 0.0 copy-start.5
  5.7 0.9 %copy-done.5 = f32[2,256,128]{2,1,0:T(8,128)S(1)} copy-done((f32[2,256,128]{2,1,0:T(8,128)S(1)}, f32[2,256,128]{2,1,0:T(8,128)}, u32[]{:S(2)}) %copy-start.5) | copy-done | bytes 262168
  6.6 0.0 copy-start.6
  6.6 0.9 %copy-done.6 = f32[8,40,72]{2,1,0:T(8,128)S(1)} copy-done((f32[8,40,72]{2,1,0:T(8,128)S(1)}, f32[8,40,72]{2,1,0:T(8,128)}, u32[]{:S(2)}) %copy-start.6) | copy-done | bytes 92184
  7.5 0.0 copy-start.7
  7.5 0.9 %copy-done.7 = f32[2,128,128]{2,1,0:T(8,128)S(1)} copy-done((f32[2,128,128]{2,1,0:T(8,128)S(1)}, f32[2,128,128]{2,1,0:T(8,128)}, u32[]{:S(2)}) %copy-start.7) | copy-done | bytes 131096
  8.4 0.0 copy-start.8
  8.4 0.7 %copy-done.8 = f32[6144]{0:T(1024)S(1)} copy-done((f32[6144]{0:T(1024)S(1)}, f32[6144]{0:T(1024)}, u32[]{:S(2)}) %copy-start.8) | copy-done | bytes 24600
  9.2 0.0 copy-start.9
  9.2 0.7 %copy-done.9 = f32[384]{0:T(512)S(1)} copy-done((f32[384]{0:T(512)S(1)}, f32[384]{0:T(512)}, u32[]{:S(2)}) %copy-start.9) | copy-done | bytes 1560
  9.8 53.8 %shard_map.136 = f32[4,256,256]{2,1,0:T(8,128)S(1)} custom-call(f32[4,256,256]{2,1,0:T(8,128)S(1)} %copy-done.1, f32[8,136,264]{2,1,0:T(8,128)} %constant.26.clone.refs_1_, f32[8,72,136]{2,1,0:T(8,128)S(1)} %copy-done.3, f32[8,40,72]{2,1,0:T(8,128)S(1)} %copy-done.6, f32[32,384,256]{2,1,0:T(8,128)} %constant.29.clone.refs_4_, ...), custom_call_target="tpu_custom_call" | custom-call | tf_op jit(solution)/shard_map/pallas_call | solution.py:387
  63.6 1.0 %copy.16 = f32[4,256,256]{2,1,0:T(8,128)} copy(f32[4,256,256]{2,1,0:T(8,128)S(1)} %shard_map.136) | data formatting | bytes 2097152
Async XLA Ops:
  0.0 1.3 %copy-start = (f32[32,3,8,384]{3,2,1,0:T(8,128)S(1)}, f32[32,3,8,384]{3,2,1,0:T(8,128)}, u32[]{:S(2)}) copy-start(f32[32,3,8,384]{3,2,1,0:T(8,128)} %constant.36.clone.refs_11_) | copy-start | bytes 3538948
  1.3 1.2 %copy-start.1 = (f32[4,256,256]{2,1,0:T(8,128)S(1)}, f32[4,256,256]{2,1,0:T(8,128)}, u32[]{:S(2)}) copy-start(f32[4,256,256]{2,1,0:T(8,128)} %refs_0_.1) | copy-start | bytes 3145732
  2.5 1.1 %copy-start.2 = (f32[2,384,256]{2,1,0:T(8,128)S(1)}, f32[2,384,256]{2,1,0:T(8,128)}, u32[]{:S(2)}) copy-start(f32[2,384,256]{2,1,0:T(8,128)} %constant.32.clone.refs_7_) | copy-start | bytes 2359300
  3.6 1.1 %copy-start.3 = (f32[8,72,136]{2,1,0:T(8,128)S(1)}, f32[8,72,136]{2,1,0:T(8,128)}, u32[]{:S(2)}) copy-start(f32[8,72,136]{2,1,0:T(8,128)} %constant.27.clone.refs_2_) | copy-start | bytes 940036
  4.7 1.0 %copy-start.4 = (f32[8,3,8,384]{3,2,1,0:T(8,128)S(1)}, f32[8,3,8,384]{3,2,1,0:T(8,128)}, u32[]{:S(2)}) copy-start(f32[8,3,8,384]{3,2,1,0:T(8,128)} %constant.35.clone.refs_10_) | copy-start | bytes 884740
  5.7 0.9 %copy-start.5 = (f32[2,256,128]{2,1,0:T(8,128)S(1)}, f32[2,256,128]{2,1,0:T(8,128)}, u32[]{:S(2)}) copy-start(f32[2,256,128]{2,1,0:T(8,128)} %constant.33.clone.refs_8_) | copy-start | bytes 786436
  6.6 0.9 %copy-start.6 = (f32[8,40,72]{2,1,0:T(8,128)S(1)}, f32[8,40,72]{2,1,0:T(8,128)}, u32[]{:S(2)}) copy-start(f32[8,40,72]{2,1,0:T(8,128)} %constant.28.clone.refs_3_) | copy-start | bytes 276484
  7.5 0.9 %copy-start.7 = (f32[2,128,128]{2,1,0:T(8,128)S(1)}, f32[2,128,128]{2,1,0:T(8,128)}, u32[]{:S(2)}) copy-start(f32[2,128,128]{2,1,0:T(8,128)} %constant.34.clone.refs_9_) | copy-start | bytes 393220
  8.4 0.7 %copy-start.8 = (f32[6144]{0:T(1024)S(1)}, f32[6144]{0:T(1024)}, u32[]{:S(2)}) copy-start(f32[6144]{0:T(1024)} %constant.38.clone.refs_13_) | copy-start | bytes 73732
  9.2 0.7 %copy-start.9 = (f32[384]{0:T(512)S(1)}, f32[384]{0:T(512)}, u32[]{:S(2)}) copy-start(f32[384]{0:T(512)} %constant.37.clone.refs_12_) | copy-start | bytes 4612

commit v2 on v1

v2 whole, which is shorter than its diff:
```python
import functools

import jax
import jax.numpy as jnp
import numpy as np
from jax import lax
from jax.experimental import pallas as pl
from jax.experimental.pallas import tpu as pltpu
from jax.sharding import PartitionSpec as P

LEVELS = 3
DEPTH = 4
LENGTH = 64.0
MESH = pl.DeviceIdType.MESH
TABLE_LANES = 384


def padded_rows(count):
    return count + 8


def padded_lanes(count):
    return (count // 128 + 1) * 128 if count >= 128 else 128


def solver_line(count):
    off = 1.0 / (3.0 * LENGTH) - LENGTH
    inner = 4.0 / (3.0 * LENGTH) + 2.0 * LENGTH
    end = 2.0 / (3.0 * LENGTH) + LENGTH
    diag = np.full(count, inner)
    diag[0] = diag[-1] = end
    q = np.ones(count)
    p = np.ones(count)
    q[1] = -diag[0] / off
    p[-2] = -diag[-1] / off
    for i in range(1, count - 1):
        q[i + 1] = -(diag[i] * q[i]) / off - q[i - 1]
        j = count - 1 - i
        p[j - 1] = -(diag[j] * p[j]) / off - p[j + 1]
    return q, p, diag[0] * p[0] + off * p[1]


def load_block(total, coarse_ids, fine_ids):
    out = np.zeros((len(coarse_ids), len(fine_ids)))

    def mass(i, j):
        if i < 0 or i >= total or j < 0 or j >= total:
            return 0.0
        if i == j:
            return (2.0 if i in (0, total - 1) else 4.0) / 6.0
        return 1.0 / 6.0 if abs(i - j) == 1 else 0.0

    for a, k in enumerate(coarse_ids):
        if k < 0 or k >= total // 2:
            continue
        upper = 1.0 if 2 * k + 1 == total - 1 else 0.5
        for b in range(max(0, 2 * k - 2 - fine_ids[0]), min(len(fine_ids), 2 * k + 3 - fine_ids[0])):
            j = fine_ids[b]
            out[a, b] = mass(2 * k, j) + 0.5 * mass(2 * k - 1, j) + upper * mass(2 * k + 1, j)
    return out


def line_tables(total, tiles):
    n = total // tiles
    h = n // 2
    coarse = total // 2
    q, p, w = solver_line(coarse)
    local, functional, carry, weight, select = [], [], [], [], []
    for t in range(tiles):
        first = t * h
        last_tile = t == tiles - 1
        ids = np.arange(first, first + h + 1)
        if last_tile:
            ids[h] = ids[h - 2]
        window = np.arange(first - 1, first + h + 2)
        load = load_block(total, window, np.arange(t * n, t * n + n + 1))
        inside = (window >= 0) & (window < coarse)
        safe = np.clip(window, 0, coarse - 1)
        low = np.minimum(ids[:, None], safe[None, :])
        high = np.maximum(ids[:, None], safe[None, :])
        green = np.where(inside[None, :], q[low] * p[high] / w, 0.0)
        local.append(green @ load)
        q_end = q[min(first + h, coarse - 1)]
        to_right = (np.where(inside, q[safe] / q_end, 0.0)) @ load
        to_left = (np.where(inside, p[safe] / p[first], 0.0)) @ load
        to_right[n] = 0.0
        to_left[0] = 0.0
        functional.append(np.stack([to_right, to_left]))
        carry.append(np.stack([p[ids] / p[first], q[ids] / q_end]))
        weights = np.zeros((2, tiles))
        for k in range(1, tiles):
            s = (t - k) % tiles
            if s < t:
                weights[0, k] = q[(s + 1) * h] * p[first] / w
            else:
                weights[1, k] = q_end * p[s * h] / w
        weight.append(weights)
        pick = np.zeros((n + 1, h + 1))
        pick[2 * np.arange(h), np.arange(h)] = 1.0
        pick[n - 4 if last_tile else n, h] = 1.0
        select.append(pick)
    return [np.stack(item) for item in (local, functional, carry, weight, select)]


def fit(array, shape):
    out = np.zeros(array.shape[: array.ndim - len(shape)] + tuple(shape))
    out[tuple(slice(0, size) for size in array.shape)] = array
    return out


def interpolation(nodes):
    out = np.eye(nodes)
    for i in range(1, nodes, 2):
        out[i] = 0.0
        out[i, i - 1] = out[i, i + 1] = 0.5
    return out


def pair_weights(weight):
    tiles = weight.shape[0]
    out = np.zeros((tiles, tiles, 2, 2))
    for t in range(tiles):
        for k in range(1, tiles):
            for way in range(2):
                out[t, (t - k) % tiles, way, way] = weight[t, way, k]
    return out


def joined_weights(first, couplings, second):
    tiles = first.shape[0]
    blocks = [first]
    blocks += [np.einsum("tsab,sbc,sucd->tuad", second, k, first) for k in couplings]
    blocks.append(second)
    out = np.zeros((tiles, 4, 2, DEPTH, tiles, 2, DEPTH))
    for t in range(tiles):
        for slot in range(tiles):
            for d in range(DEPTH):
                for i, block in enumerate(blocks):
                    out[t, i, :, d, slot, :, d] = block[t, (t - slot) % tiles]
    return out.reshape(tiles, 32, tiles * 8)


@functools.lru_cache(maxsize=None)
def tables(nx, ny, gx, gy):
    row_vecs = np.zeros((gx, LEVELS, 8, TABLE_LANES))
    col_vecs = np.zeros((gy, LEVELS, 8, TABLE_LANES))
    mats, sides = ([], [], []), []
    weights = []
    for vecs, size, tiles in ((row_vecs, nx, gx), (col_vecs, ny, gy)):
        lines = [line_tables(size >> level, tiles) for level in range(LEVELS)]
        sides.append(lines)
        for level, (local, functional, carry, weight, select) in enumerate(lines):
            n = (size >> level) // tiles
            h = n // 2
            vecs[:, level, 0:2, : n + 1] = functional
            vecs[:, level, 2:4, : h + 1] = carry
            if vecs is row_vecs:
                mats[0].append(fit(local, (padded_rows(h), padded_rows(n))))
            else:
                shape = (padded_lanes(n), padded_lanes(h))
                joined = np.concatenate([local, functional], axis=1).transpose(0, 2, 1)
                mats[1].append(fit(joined, shape))
                mats[2].append(fit(select[[0, -1]], shape))
        weights.append(lines[0][3])
    nodes = (nx // gx >> 2) + 1
    inter = interpolation(nodes)
    rest = np.eye(nodes) - inter
    (_, _, carry_a, weight_a, _), (local_b, func_b, carry_b, weight_b, _) = sides[0][1:]
    row_k = [np.einsum("tbi,ij,taj->tba", func_b, op, carry_a) for op in (rest, inter)]
    row_join = joined_weights(pair_weights(weight_a), row_k, pair_weights(weight_b))
    row_after = np.zeros((gx, 256, 128))
    half = carry_b.shape[2]
    for i, op in enumerate((rest, inter)):
        row_vecs[:, 1, 4 + 2 * i : 6 + 2 * i, :nodes] = func_b @ op
        row_vecs[:, 2, 4 + 2 * i : 6 + 2 * i, :half] = np.einsum("tij,taj->tai", local_b @ op, carry_a)
        row_after[:, 128 * i : 128 * i + nodes, :half] = (local_b @ op).transpose(0, 2, 1)
        row_after[:, 128 * i + nodes + 2 * i : 128 * i + nodes + 2 * i + 2, :half] = carry_b
    (_, _, carry_a, weight_a, _), (local_b, func_b, _, weight_b, _) = sides[1][1:]
    col_k = [np.einsum("tbi,ij,taj->tba", func_b, op, carry_a) for op in (np.eye(nodes), rest)]
    col_join = joined_weights(pair_weights(weight_a), col_k, pair_weights(weight_b))
    col_after = np.zeros((gy, 256, 128))
    col_vecs[:, 1, 4:6, :nodes] = func_b @ rest
    both = np.concatenate([local_b, func_b], axis=1)
    for i, op in enumerate((np.eye(nodes), rest)):
        col_vecs[:, 2, 4 + 2 * i : 6 + 2 * i, :half] = np.einsum("tij,taj->tai", local_b @ op, carry_a)
        col_after[:, 128 * i : 128 * i + nodes, : both.shape[1]] = (both @ op).transpose(0, 2, 1)
    as32 = lambda item: np.ascontiguousarray(item, np.float32)
    grids = mats[0] + mats[1] + mats[2] + [row_join, row_after, col_join, col_after, row_vecs, col_vecs]
    return [as32(m) for m in grids], [as32(w.reshape(-1)) for w in weights]


def parts(value, count):
    out = []
    for _ in range(count):
        out.append(value.astype(jnp.bfloat16))
        value = value - out[-1].astype(jnp.float32)
    return out


def dot(a, b, dims=((1,), (0,))):
    return lax.dot_general(
        a, b, (dims, ((), ())), precision=lax.Precision.HIGHEST, preferred_element_type=jnp.float32
    )


def pick_dot(a, b, count=3, dims=((1,), (0,)), ones=1):
    total = None
    for part in reversed(parts(b if ones == 0 else a, count)):
        x, y = (a.astype(jnp.bfloat16), part) if ones == 0 else (part, b.astype(jnp.bfloat16))
        term = lax.dot_general(x, y, (dims, ((), ())), preferred_element_type=jnp.float32)
        total = term if total is None else total + term
    return total


def iota(shape, dim):
    return lax.broadcasted_iota(jnp.int32, shape, dim)


def detail(u):
    rows, lanes = u.shape
    odd_lane = iota(u.shape, 1) % 2 == 1
    odd_row = iota(u.shape, 0) % 2 == 1
    along = jnp.where(odd_lane, 0.5 * (pltpu.roll(u, 1, 1) + pltpu.roll(u, lanes - 1, 1)), u)
    both = jnp.where(odd_row, 0.5 * (pltpu.roll(along, 1, 0) + pltpu.roll(along, rows - 1, 0)), along)
    return u - both


def spread_matrix(count, lanes, stride, width):
    shape = (lanes, width)
    row = iota(shape, 0)
    return jnp.where((iota(shape, 1) == stride * row) & (row < count), 1.0, 0.0).astype(jnp.float32)


def kernel(gx_n, gy_n, n0, *refs):
    sal, out = refs[0], refs[18]
    tables_in, (row_w, col_w) = refs[1:16], refs[16:18]
    (u0, u1, w0, w1, out_v, tall_v) = refs[19:25]
    tables_v = refs[25:40]
    (hrow, hcol, hcorner, hrow_in, hcol_in, hcorner_in, xs0, xr0, ys0, yr0, xs1, xr1, ys1, yr1,
     load_sem, halo_send, halo_recv, x_send, x_recv, y_send, y_recv, out_sem) = refs[40:]
    row_mats, col_mats, selects = tables_v[0:3], tables_v[3:6], tables_v[6:9]
    row_join, row_after, col_join, col_after, rv, cv = tables_v[9:15]
    gx, gy = lax.axis_index("gx"), lax.axis_index("gy")
    last_x, last_y = gx == gx_n - 1, gy == gy_n - 1
    is_last_col = (gy + 1) // gy_n

    loads = [pltpu.make_async_copy(sal, u0.at[:, pl.ds(0, n0), pl.ds(0, n0)], load_sem.at[0])]
    places = [gx] * 3 + [gy] * 3 + [is_last_col] * 3 + [gx, gx, gy, gy, gx, gy]
    later = [(dst, src.at[place]) for dst, src, place in zip(tables_v, tables_in, places)]
    for i, (dst, src) in enumerate(later):
        loads.append(pltpu.make_async_copy(src, dst, load_sem.at[1 + i]))
    for copy in loads:
        copy.start()

    barrier = pltpu.get_barrier_semaphore()
    x_peers = [(lax.rem(gx + k, gx_n), gy) for k in range(1, gx_n)]
    y_peers = [(gx, lax.rem(gy + k, gy_n)) for k in range(1, gy_n)]
    up, left = lax.rem(gx + gx_n - 1, gx_n), lax.rem(gy + gy_n - 1, gy_n)
    greeted = x_peers + y_peers + [(lax.rem(gx + 1, gx_n), lax.rem(gy + 1, gy_n))]
    for peer in greeted:
        pl.semaphore_signal(barrier, inc=1, device_id=peer, device_id_type=MESH)

    loads[0].wait()
    edge = jnp.where(iota((DEPTH, n0), 1) == 0, 1.0, 0.0)
    depth_row = iota((DEPTH, n0), 0)
    hrow[...] = u0[:, 0, 0:n0]
    hcorner[...] = u0[:, 0, 0:128]
    first_cols = jnp.zeros((DEPTH, n0), jnp.float32)
    for d in range(DEPTH):
        first_cols += pick_dot(jnp.where(depth_row == d, edge, 0.0), u0[d, 0:n0, 0:n0], 3, ((1,), (1,)), 0)
    hcol[...] = first_cols
    pl.semaphore_wait(barrier, len(greeted))
    halos = []
    for i, (src, dst, peer) in enumerate(
        ((hrow, hrow_in, (up, gy)), (hcol, hcol_in, (gx, left)), (hcorner, hcorner_in, (up, left)))
    ):
        copy = pltpu.make_async_remote_copy(
            src_ref=src, dst_ref=dst, send_sem=halo_send.at[i], recv_sem=halo_recv.at[i],
            device_id=peer, device_id_type=MESH,
        )
        copy.start()
        halos.append(copy)
    for copy in loads[1:]:
        copy.wait()
    for copy in halos:
        copy.wait_recv()
    lane0 = iota((n0, 128), 1) == 0
    first_row = iota((8, 1), 0) == 0
    cols_in = jnp.concatenate([hcol_in[...], jnp.zeros((4, n0), jnp.float32)], axis=0).T
    for d in range(DEPTH):
        own_alias = u0[d, 0:n0, n0 - 2 : n0 - 1]
        column = jnp.where(last_y, own_alias, cols_in[:, d : d + 1])
        u0[d, 0:n0, n0 : n0 + 128] = jnp.where(lane0, column, 0.0)
        row = jnp.where(last_x, u0[d, n0 - 2 : n0 - 1, 0:n0], hrow_in[d : d + 1, :])
        corner = jnp.where(
            last_y,
            row[:, n0 - 2 : n0 - 1],
            jnp.where(last_x, u0[d, n0 - 2 : n0 - 1, n0 : n0 + 1], hcorner_in[d : d + 1, 0:1]),
        )
        u0[d, n0 : n0 + 8, 0:n0] = jnp.where(first_row, row, 0.0)
        u0[d, n0 : n0 + 8, n0 : n0 + 128] = jnp.where(first_row & (iota((8, 128), 1) == 0), corner, 0.0)

    def send_all(peers, me, count, src, dst, send, recv):
        for k, peer in enumerate(peers):
            pltpu.make_async_remote_copy(
                src_ref=src.at[(me + k + 1) // count], dst_ref=dst.at[k], send_sem=send, recv_sem=recv,
                device_id=peer, device_id_type=MESH,
            ).start()

    def send_same(peers, src, dst, send, recv):
        for k, peer in enumerate(peers):
            pltpu.make_async_remote_copy(
                src_ref=src, dst_ref=dst.at[k + 1], send_sem=send, recv_sem=recv, device_id=peer, device_id_type=MESH
            ).start()

    def gather(buf, weights, base, count):
        right = jnp.zeros(buf.shape[1:], jnp.float32)
        left_sum = jnp.zeros(buf.shape[1:], jnp.float32)
        for k in range(1, count):
            part = buf[k - 1]
            right += weights[base + k] * part
            left_sum += weights[base + count + k] * part
        return right, left_sum

    def local_level(level, n, u, w):
        h = n // 2
        rows, rows_c, lanes_c = padded_rows(n), padded_rows(h), padded_lanes(h)
        col_mat, row_mat, select = col_mats[level][...], row_mats[level][...], selects[level][...]
        base, across, solved, cols_local = [], [], [], jnp.zeros((8, rows_c), jnp.float32)
        row8, lane8 = iota((8, lanes_c), 0), iota((8, lanes_c), 1)
        is_tail = iota((rows_c, lanes_c), 0) == h
        for d in range(DEPTH):
            q = dot(w[d], col_mat)
            z = dot(row_mat, q)
            pick = ((row8 == d) & (lane8 == h + 1)) | ((row8 == 4 + d) & (lane8 == h + 2))
            cols_local += pick_dot(jnp.where(pick, 1.0, 0.0), z, 3, ((1,), (1,)), 0)
            even = even_rows(tall_v, pick_dot(u[d], select), rows_c)
            even = jnp.where(is_tail & last_x, even[h - 2 : h - 1, :], even)
            base.append(jnp.where(iota((rows_c, lanes_c), 1) <= h, z, 0.0) + even)
            across.append(q)
            solved.append(z)
        tall = padded_lanes(h)
        if rows_c < tall:
            cols_local = jnp.concatenate([cols_local, jnp.zeros((8, tall - rows_c), jnp.float32)], axis=1)
        return base, across, solved, cols_local

    def row_sums(values, weights):
        sums = []
        for way in range(2):
            for d in range(DEPTH):
                rows = values[d].shape[0]
                sums.append(jnp.sum(values[d] * weights[0:rows, way : way + 1], axis=0, keepdims=True))
        return jnp.concatenate(sums, axis=0)

    def line(value, functional):
        return jnp.sum(value * functional, axis=1, keepdims=True)

    def twice(table, row, lanes):
        return jnp.concatenate(
            [jnp.broadcast_to(table[row + way : row + way + 1, 0:lanes], (4, lanes)) for way in range(2)], axis=0
        )

    def outer(column, table, row, lanes):
        return (
            column[0:4] * table[row : row + 1, 0:lanes] + column[4:8] * table[row + 1 : row + 2, 0:lanes]
        )

    def spread_out(values, count, lanes, stride, pieces):
        mat = spread_matrix(count, lanes, stride, n0)
        for d in range(DEPTH):
            add_rows(out_v, d, pick_dot(values[d][0:count], mat, pieces), stride)

    n, h = n0, n0 // 2
    lanes, rows_c, lanes_c = padded_lanes(n), padded_rows(h), padded_lanes(h)
    for d in range(DEPTH):
        w0[d] = detail(u0[d])
    sums = row_sums([w0[d] for d in range(DEPTH)], rv[0].T)
    xs0[0] = sums[0:4]
    xs0[1] = sums[4:8]
    send_all(x_peers, gx, gx_n, xs0, xr0, x_send.at[0], x_recv.at[0])
    base, _, _, cols_local = local_level(0, n, u0, w0)
    pltpu.make_async_copy(xr0, xr0, x_recv.at[0]).wait()
    a_right, a_left = gather(xr0, row_w, gx * 2 * gx_n, gx_n)
    q_r, q_l = cv[0, 0:1, 0:lanes], cv[0, 1:2, 0:lanes]
    p_r, p_l = rv[0, 2:3, 0:lanes_c], rv[0, 3:4, 0:lanes_c]
    ys0[0] = cols_local[0:4] + line(a_right, q_r) * p_r + line(a_left, q_r) * p_l
    ys0[1] = cols_local[4:8] + line(a_right, q_l) * p_r + line(a_left, q_l) * p_l
    send_all(y_peers, gy, gy_n, ys0, yr0, y_send.at[0], y_recv.at[0])
    for d in range(DEPTH):
        for j in range(out_v.shape[1]):
            out_v[d, j] = w0[d, 0:n0, 128 * j : 128 * j + 128]
    carried = dot(jnp.concatenate([a_right, a_left], axis=0), col_mats[0][...])
    carried = jnp.where(iota((8, lanes_c), 1) <= h, carried, 0.0)
    other = jnp.concatenate([carried, twice(cv[0], 2, lanes_c)], axis=0)
    own = twice(rv[0], 2, lanes_c)
    pltpu.make_async_copy(yr0, yr0, y_recv.at[0]).wait()
    c_right, c_left = gather(yr0, col_w, gy * 2 * gy_n, gy_n)
    lhs = jnp.concatenate([own, c_right, c_left], axis=0).T[0:rows_c]
    for d in range(DEPTH):
        u1[d] = base[d] + dot(lhs, jnp.where(iota((16, lanes_c), 0) % 4 == d, other, 0.0))

    n, h, g = n0 // 2, n0 // 4, n0 // 8
    for d in range(DEPTH):
        w1[d] = detail(u1[d])
    rv1 = rv[1, :, 0 : 2 * 128].T
    rv2 = rv[2, :, 0:128].T
    base1, across1, solved1, cols1 = local_level(1, n, u1, w1)
    base2_w = [detail(base1[d]) for d in range(DEPTH)]
    _, across2, _, cols2 = local_level(2, h, base1, base2_w)
    lane = iota((8, 128), 1)
    is_c = (lane == h + 1) | (lane == h + 2)
    sent = row_sums(across1, rv1) + pltpu.roll(row_sums(across2, rv2), h + 3, 1)
    for i in range(2):
        of_cols = row_sums(solved1, rv1[:, 4 + 2 * i : 6 + 2 * i])
        sent += pltpu.roll(jnp.where(is_c, of_cols, 0.0), g + 5 + 2 * i, 1)
    xs1[...] = sent
    xr1[0] = sent
    send_same(x_peers, xs1, xr1, x_send.at[1], x_recv.at[1])
    spread_out([w1[d] for d in range(DEPTH)], n, 256, 2, 2)
    others = xr1.at[pl.ds(1, gx_n - 1)]
    pltpu.make_async_copy(others, others, x_recv.at[1]).wait()
    got = dot(row_join[...], xr1[...].reshape(gx_n * 8, 128))
    a_1 = got[0:8]
    a_2 = pltpu.roll(got[24:32], 128 - (h + 3), 1) + dot(
        jnp.concatenate([got[8:16], got[16:24]], axis=1), col_after[...]
    )
    kappa = got[0:8]
    msg, msg2, hs = [], [], []
    for way in range(2):
        msg.append(cols1[4 * way : 4 * way + 4] + outer(kappa[:, h + 1 + way : h + 2 + way], rv[1], 2, 128))
        row = outer(line(a_1, cv[2, way : way + 1, 0:128]), rv[2], 4, 128)
        row += outer(line(a_1, cv[1, 4 + way : 5 + way, 0:128]), rv[2], 6, 128)
        row += outer(a_2[:, g + 1 + way : g + 2 + way], rv[2], 2, 128)
        msg2.append(cols2[4 * way : 4 * way + 4] + row)
        block = jnp.zeros((4, 128), jnp.float32)
        for i in range(2):
            at = h + g + 6 + 2 * i + way
            h_col = got[24:32, at : at + 1] + got[8 + 8 * i : 16 + 8 * i, h + 1 + way : h + 2 + way]
            for x_way in range(2):
                block += jnp.where(iota((4, 128), 1) == h + 1 + 2 * i + x_way, h_col[4 * x_way : 4 * x_way + 4], 0.0)
        hs.append(block)
    sent = jnp.concatenate(msg, axis=0) + pltpu.roll(jnp.concatenate(msg2, axis=0), h + 5, 1)
    sent += jnp.concatenate(hs, axis=0)
    ys1[...] = sent
    yr1[0] = sent
    send_same(y_peers, ys1, yr1, y_send.at[1], y_recv.at[1])
    lane = iota((8, 128), 1)
    carried1 = jnp.where(lane <= h, a_1, 0.0)
    other1 = jnp.concatenate([carried1, twice(cv[1], 2, 128)], axis=0)
    others = yr1.at[pl.ds(1, gy_n - 1)]
    pltpu.make_async_copy(others, others, y_recv.at[1]).wait()
    got = dot(col_join[...], yr1[...].reshape(gy_n * 8, 128))
    c_1 = jnp.where(lane <= h, got[0:8], 0.0)
    c_2 = pltpu.roll(got[24:32], 128 - (h + 5), 1) + dot(
        jnp.concatenate([got[8:16], got[16:24]], axis=1), row_after[...]
    )
    lhs = jnp.concatenate([twice(rv[1], 2, 128), c_1], axis=0).T[0 : padded_rows(h)]
    nodes, details = [], []
    for d in range(DEPTH):
        nodes.append(base1[d] + dot(lhs, jnp.where(iota((16, 128), 0) % 4 == d, other1, 0.0)))
        details.append(detail(nodes[d]))
    base2, _, _, _ = local_level(2, h, nodes, details)
    extra = []
    for x_way in range(2):
        part = jnp.zeros((4, 128), jnp.float32)
        for i in range(2):
            part += outer(got[0:8, h + 1 + 2 * i + x_way : h + 2 + 2 * i + x_way], cv[2], 4 + 2 * i, 128)
        extra.append(part)
    carried2 = jnp.where(lane <= g, a_2, 0.0) + jnp.concatenate(extra, axis=0)
    other2 = jnp.concatenate([carried2, twice(cv[2], 2, 128)], axis=0)
    c_2 = jnp.where(lane <= g, c_2, 0.0)
    lhs = jnp.concatenate([twice(rv[2], 2, 128), c_2], axis=0).T[0 : padded_rows(g)]
    last = []
    for d in range(DEPTH):
        last.append(base2[d] + dot(lhs, jnp.where(iota((16, 128), 0) % 4 == d, other2, 0.0)))
    spread_out(details, h, 128, 4, 2)
    spread_out(last, g, 128, 8, 3)

    results = []
    for j in range(out_v.shape[1]):
        results.append(pltpu.make_async_copy(out_v.at[:, j], out.at[:, :, pl.ds(128 * j, 128)], out_sem.at[j]))
        results[-1].start()
    for i, copy in enumerate(halos):
        copy.wait_send()
    pltpu.make_async_copy(xr0, xr0, x_send.at[0]).wait()
    pltpu.make_async_copy(yr0, yr0, y_send.at[0]).wait()
    others = xr1.at[pl.ds(1, gx_n - 1)]
    pltpu.make_async_copy(others, others, x_send.at[1]).wait()
    others = yr1.at[pl.ds(1, gy_n - 1)]
    pltpu.make_async_copy(others, others, y_send.at[1]).wait()
    for copy in results:
        copy.wait()


def even_rows(tall_v, value, rows_c):
    rows, lanes = value.shape
    half = rows // 2
    parts = []
    for j in range(lanes // 128):
        tall_v[j, 0:rows] = value[:, 128 * j : 128 * j + 128]
        part = tall_v[j, pl.ds(0, half, stride=2), :]
        parts.append(jnp.concatenate([part, jnp.zeros((rows_c - half, 128), jnp.float32)], axis=0))
    return jnp.concatenate(parts, axis=1)


def add_rows(ref, d, value, stride):
    place = pl.ds(0, value.shape[0], stride=stride)
    for j in range(ref.shape[1]):
        ref[d, j, place, :] = ref[d, j, place, :] + value[:, 128 * j : 128 * j + 128]


def shards(salinity):
    gx_n, gy_n = lax.axis_size("gx"), lax.axis_size("gy")
    _, nx, ny = salinity.shape
    n0 = nx
    grids, weights = tables(nx * gx_n, ny * gy_n, gx_n, gy_n)
    vmem = lambda *shape: pltpu.VMEM(shape, jnp.float32)
    dma = lambda count: pltpu.SemaphoreType.DMA((count,))
    wide, wide_c = padded_lanes(n0), padded_lanes(n0 // 2)
    levels = [vmem(DEPTH, padded_rows(n), padded_lanes(n)) for n in (n0, n0 // 2)]
    scratch = levels + levels + [vmem(DEPTH, n0 // 128, n0, 128), vmem(2, padded_rows(n0), 128)]
    scratch += [vmem(*m.shape[1:]) for m in grids]
    scratch += [vmem(DEPTH, n0), vmem(DEPTH, n0), vmem(DEPTH, 128)] * 2
    scratch += [vmem(2, DEPTH, wide), vmem(gx_n - 1, DEPTH, wide)]
    scratch += [vmem(2, DEPTH, wide_c), vmem(gy_n - 1, DEPTH, wide_c)]
    scratch += [vmem(8, 128), vmem(gx_n, 8, 128), vmem(8, 128), vmem(gy_n, 8, 128)]
    scratch += [dma(1 + len(grids)), dma(3), dma(3), dma(2), dma(2), dma(2), dma(2), dma(n0 // 128)]
    anywhere = pl.BlockSpec(memory_space=pl.ANY)
    scalars = pl.BlockSpec(memory_space=pltpu.SMEM)
    return pl.pallas_call(
        functools.partial(kernel, gx_n, gy_n, n0),
        out_shape=jax.ShapeDtypeStruct(salinity.shape, jnp.float32),
        in_specs=[anywhere] * (1 + len(grids)) + [scalars] * 2,
        out_specs=anywhere,
        scratch_shapes=scratch,
        compiler_params=pltpu.CompilerParams(
            collective_id=0, has_side_effects=True, vmem_limit_bytes=63 * 1024 * 1024
        ),
    )(salinity, *grids, *weights)


def solution(mesh):
    placed = P(None, "gx", "gy")
    return jax.shard_map(shards, mesh=mesh, in_specs=(placed,), out_specs=placed, check_vma=False)
```

time: 65 us -> 50.4 us (0.78)
  local copies, waits for them, and re-layouts: 10.8 us -> 2.29 us
  Pallas kernels: 53.8 us -> 47.9 us
    unnamed x21 -> x1, local copies, waits for them, and re-layouts: 10.8 us -> 2.29 us
    pallas_call x1, Pallas kernels: 53.8 us -> 47.9 us  [shards(): pl.pallas_call(functools.partial(kernel, gx_n, gy_n, n0), out_shape=jax.S...]
where the time goes in v2:
time: 50.4 us; the launch traced here: 50.2 us
  Pallas kernels  47.9 us (95%)
  local copies, waits for them, and re-layouts  2.29 us (5%)
    pallas_call x1, Pallas kernels, shards(): pl.pallas_call(functools.partial(kernel, gx_n, gy_n, n0), out_shape=jax.S...  47.9 us
    unnamed x1, local copies, waits for them, and re-layouts  2.29 us

profile of v2, /device:TPU:1, one launch (start us, length us, event | category | flops | bytes accessed | tf_op | source)
XLA Modules:
  0.0 50.2 jit_solution(17490300057443069787)
XLA Ops:
  0.0 47.9 %shard_map.172 = f32[4,256,256]{2,1,0:T(8,128)} custom-call(f32[4,256,256]{2,1,0:T(8,128)} %refs_0_.1, f32[8,136,264]{2,1,0:T(8,128)} %constant.34.clone.refs_1_, f32[8,72,136]{2,1,0:T(8,128)} %constant.35.clone.refs_2_, f32[8,40,72]{2,1,0:T(8,128)} %constant.36.clone.refs_3_, f32[32,384,256]{2,1,0:T(8,128)} %constant.37.clone.refs_4_, ...), custom_call_target="tpu_custom_call" | custom-call | tf_op jit(solution)/shard_map/pallas_call | solution.py:530
  47.9 2.3 %copy.20 = f32[4,256,256]{2,1,0:T(8,128)} copy(f32[4,256,256]{2,1,0:T(8,128)} %shard_map.172) | data formatting | bytes 2097152

commit v3 on v2

v3 whole, which is shorter than its diff:
```python
import functools

import jax
import jax.numpy as jnp
import numpy as np
from jax import lax
from jax.experimental import pallas as pl
from jax.experimental.pallas import tpu as pltpu
from jax.sharding import PartitionSpec as P

LEVELS = 3
DEPTH = 4
LENGTH = 64.0
MESH = pl.DeviceIdType.MESH
TABLE_LANES = 384
VMEM_LIMIT = 52 * 1024 * 1024


def padded_rows(count):
    return count + 8


def padded_lanes(count):
    return (count // 128 + 1) * 128 if count >= 128 else 128


def solver_line(count):
    off = 1.0 / (3.0 * LENGTH) - LENGTH
    inner = 4.0 / (3.0 * LENGTH) + 2.0 * LENGTH
    end = 2.0 / (3.0 * LENGTH) + LENGTH
    diag = np.full(count, inner)
    diag[0] = diag[-1] = end
    q = np.ones(count)
    p = np.ones(count)
    q[1] = -diag[0] / off
    p[-2] = -diag[-1] / off
    for i in range(1, count - 1):
        q[i + 1] = -(diag[i] * q[i]) / off - q[i - 1]
        j = count - 1 - i
        p[j - 1] = -(diag[j] * p[j]) / off - p[j + 1]
    return q, p, diag[0] * p[0] + off * p[1]


def load_block(total, coarse_ids, fine_ids):
    out = np.zeros((len(coarse_ids), len(fine_ids)))

    def mass(i, j):
        if i < 0 or i >= total or j < 0 or j >= total:
            return 0.0
        if i == j:
            return (2.0 if i in (0, total - 1) else 4.0) / 6.0
        return 1.0 / 6.0 if abs(i - j) == 1 else 0.0

    for a, k in enumerate(coarse_ids):
        if k < 0 or k >= total // 2:
            continue
        upper = 1.0 if 2 * k + 1 == total - 1 else 0.5
        for b in range(max(0, 2 * k - 2 - fine_ids[0]), min(len(fine_ids), 2 * k + 3 - fine_ids[0])):
            j = fine_ids[b]
            out[a, b] = mass(2 * k, j) + 0.5 * mass(2 * k - 1, j) + upper * mass(2 * k + 1, j)
    return out


def line_tables(total, tiles):
    n = total // tiles
    h = n // 2
    coarse = total // 2
    q, p, w = solver_line(coarse)
    local, functional, carry, weight, select = [], [], [], [], []
    for t in range(tiles):
        first = t * h
        last_tile = t == tiles - 1
        ids = np.arange(first, first + h + 1)
        if last_tile:
            ids[h] = ids[h - 2]
        window = np.arange(first - 1, first + h + 2)
        load = load_block(total, window, np.arange(t * n, t * n + n + 1))
        inside = (window >= 0) & (window < coarse)
        safe = np.clip(window, 0, coarse - 1)
        low = np.minimum(ids[:, None], safe[None, :])
        high = np.maximum(ids[:, None], safe[None, :])
        green = np.where(inside[None, :], q[low] * p[high] / w, 0.0)
        local.append(green @ load)
        q_end = q[min(first + h, coarse - 1)]
        to_right = (np.where(inside, q[safe] / q_end, 0.0)) @ load
        to_left = (np.where(inside, p[safe] / p[first], 0.0)) @ load
        to_right[n] = 0.0
        to_left[0] = 0.0
        functional.append(np.stack([to_right, to_left]))
        carry.append(np.stack([p[ids] / p[first], q[ids] / q_end]))
        weights = np.zeros((2, tiles))
        for k in range(1, tiles):
            s = (t - k) % tiles
            if s < t:
                weights[0, k] = q[(s + 1) * h] * p[first] / w
            else:
                weights[1, k] = q_end * p[s * h] / w
        weight.append(weights)
        pick = np.zeros((n + 1, h + 1))
        pick[2 * np.arange(h), np.arange(h)] = 1.0
        pick[n - 4 if last_tile else n, h] = 1.0
        select.append(pick)
    return [np.stack(item) for item in (local, functional, carry, weight, select)]


def fit(array, shape):
    out = np.zeros(array.shape[: array.ndim - len(shape)] + tuple(shape))
    out[tuple(slice(0, size) for size in array.shape)] = array
    return out


def interpolation(nodes):
    out = np.eye(nodes)
    for i in range(1, nodes, 2):
        out[i] = 0.0
        out[i, i - 1] = out[i, i + 1] = 0.5
    return out


def pair_weights(weight):
    tiles = weight.shape[0]
    out = np.zeros((tiles, tiles, 2, 2))
    for t in range(tiles):
        for k in range(1, tiles):
            for way in range(2):
                out[t, (t - k) % tiles, way, way] = weight[t, way, k]
    return out


def joined_weights(first, couplings, second):
    tiles = first.shape[0]
    blocks = [first]
    blocks += [np.einsum("tsab,sbc,sucd->tuad", second, k, first) for k in couplings]
    blocks.append(second)
    out = np.zeros((tiles, 4, 2, DEPTH, tiles, 2, DEPTH))
    for t in range(tiles):
        for slot in range(tiles):
            for d in range(DEPTH):
                for i, block in enumerate(blocks):
                    out[t, i, :, d, slot, :, d] = block[t, (t - slot) % tiles]
    return out.reshape(tiles, 32, tiles * 8)


def packed(tables):
    places, blocks, at = {}, [], 0
    for name, table in tables.items():
        rows, lanes = -(-table.shape[1] // 8) * 8, -(-table.shape[2] // 128) * 128
        table = fit(table, (rows, lanes))
        places[name] = (at, rows, lanes // 128)
        at += rows * (lanes // 128)
        blocks += [table[:, :, 128 * j : 128 * j + 128] for j in range(lanes // 128)]
    return np.ascontiguousarray(np.concatenate(blocks, axis=1), np.float32), places


@functools.lru_cache(maxsize=None)
def tables(nx, ny, gx, gy):
    row_vecs = np.zeros((gx, 8 * LEVELS + 8, TABLE_LANES))
    col_vecs = np.zeros((gy, 8 * LEVELS + 8, TABLE_LANES))
    row_out, col_out, sides = {}, {}, []
    for vecs, size, tiles, out in ((row_vecs, nx, gx, row_out), (col_vecs, ny, gy, col_out)):
        lines = [line_tables(size >> level, tiles) for level in range(LEVELS)]
        sides.append(lines)
        for level, (local, functional, carry, weight, select) in enumerate(lines):
            n = (size >> level) // tiles
            h = n // 2
            vecs[:, 8 * level : 8 * level + 2, : n + 1] = functional
            vecs[:, 8 * level + 2 : 8 * level + 4, : h + 1] = carry
            if vecs is row_vecs:
                out[f"mat{level}"] = fit(local, (padded_rows(h), padded_lanes(n)))
                if level == 0:
                    vecs[:, 4, : h + 1] = local[:, :, n - 1]
                    vecs[:, 5, : h + 1] = local[:, :, n]
            else:
                joined = np.concatenate([local, functional], axis=1).transpose(0, 2, 1)
                out[f"mat{level}"] = fit(joined, (padded_lanes(n), padded_lanes(h)))
        out["weight"] = np.repeat(lines[0][3].reshape(tiles, 2 * tiles, 1), 128, axis=2)
    nodes = (nx // gx >> 2) + 1
    inter = interpolation(nodes)
    rest = np.eye(nodes) - inter
    (local_a, _, carry_a, weight_a, select_a), (local_b, func_b, carry_b, weight_b, select_b) = sides[0][1:]
    row_k = [np.einsum("tbi,ij,taj->tba", func_b, op, carry_a) for op in (rest, inter)]
    row_out["join"] = joined_weights(pair_weights(weight_a), row_k, pair_weights(weight_b))
    after = np.zeros((gx, 384, 128))
    half = carry_b.shape[2]
    taken = np.zeros((gx, 8, TABLE_LANES))
    for i, op in enumerate((rest, inter)):
        func = func_b @ op
        row_vecs[:, 12 + 2 * i : 14 + 2 * i, : local_a.shape[2]] = np.einsum("tij,tjk->tik", func, local_a)
        taken[:, 2 * i : 2 * i + 2, : select_a.shape[1]] = np.einsum("tij,tkj->tik", func, select_a)
        row_vecs[:, 20 + 2 * i : 22 + 2 * i, :half] = np.einsum("tij,taj->tai", local_b @ op, carry_a)
        after[:, 128 * i : 128 * i + nodes, :half] = (local_b @ op).transpose(0, 2, 1)
        after[:, 128 * i + nodes + 2 * i : 128 * i + nodes + 2 * i + 2, :half] = carry_b
    after[:, 256 : 256 + nodes, :half] = select_b
    row_vecs[:, 24:26, :half] = carry_a @ select_b
    row_out.update(after=after, taken=taken, vecs=row_vecs)
    (_, _, carry_a, weight_a, _), (local_b, func_b, _, weight_b, select_b) = sides[1][1:]
    col_k = [np.einsum("tbi,ij,taj->tba", func_b, op, carry_a) for op in (np.eye(nodes), rest)]
    col_out["join"] = joined_weights(pair_weights(weight_a), col_k, pair_weights(weight_b))
    after = np.zeros((gy, 384, 128))
    col_vecs[:, 12:14, :nodes] = func_b @ rest
    both = np.concatenate([local_b, func_b], axis=1)
    for i, op in enumerate((np.eye(nodes), rest)):
        col_vecs[:, 20 + 2 * i : 22 + 2 * i, :half] = np.einsum("tij,taj->tai", local_b @ op, carry_a)
        after[:, 128 * i : 128 * i + nodes, : both.shape[1]] = (both @ op).transpose(0, 2, 1)
    after[:, 256 : 256 + nodes, :half] = select_b
    col_vecs[:, 24:26, :half] = carry_a @ select_b
    col_out.update(after=after, vecs=col_vecs)
    return packed(row_out), packed(col_out)


def parts(value, count):
    out = []
    for _ in range(count):
        out.append(value.astype(jnp.bfloat16))
        value = value - out[-1].astype(jnp.float32)
    return out


def dot(a, b, dims=((1,), (0,))):
    return lax.dot_general(
        a, b, (dims, ((), ())), precision=lax.Precision.HIGHEST, preferred_element_type=jnp.float32
    )


def pick_dot(a, b, count=3, dims=((1,), (0,)), ones=1):
    total = None
    for part in reversed(parts(b if ones == 0 else a, count)):
        x, y = (a.astype(jnp.bfloat16), part) if ones == 0 else (part, b.astype(jnp.bfloat16))
        term = lax.dot_general(x, y, (dims, ((), ())), preferred_element_type=jnp.float32)
        total = term if total is None else total + term
    return total


def iota(shape, dim):
    return lax.broadcasted_iota(jnp.int32, shape, dim)


def detail(u, alone=False):
    rows, lanes = u.shape
    lane, row = iota(u.shape, 1), iota(u.shape, 0)
    left, right = pltpu.roll(u, 1, 1), pltpu.roll(u, lanes - 1, 1)
    if alone:
        right = jnp.where(lane == lanes - 1, left, right)
    along = jnp.where(lane % 2 == 1, 0.5 * (left + right), u)
    above, below = pltpu.roll(along, 1, 0), pltpu.roll(along, rows - 1, 0)
    if alone:
        below = jnp.where(row == rows - 1, above, below)
    return u - jnp.where(row % 2 == 1, 0.5 * (above + below), along)


def spread_matrix(count, lanes, stride, width):
    shape = (lanes, width)
    row = iota(shape, 0)
    return jnp.where((iota(shape, 1) == stride * row) & (row < count), 1.0, 0.0).astype(jnp.float32)


def kernel(gx_n, gy_n, n0, row_places, col_places, *refs):
    (sal, row_in, col_in, out, out_v, u0, u1, w0, w1, tall_v, row_v, col_v,
     hrow, hcol, hcorner, hrow_in, hcol_in, hcorner_in, xs0, xr0, ys0, yr0, xs1, xr1, ys1, yr1,
     load_sem, halo_send, halo_recv, x_send, x_recv, y_send, y_recv) = refs

    def table(ref, places, name):
        at, rows, tiles = places[name]
        return jnp.concatenate([ref[at + j * rows : at + (j + 1) * rows] for j in range(tiles)], axis=1)

    row_table = functools.partial(table, row_v, row_places)
    col_table = functools.partial(table, col_v, col_places)
    gx, gy = lax.axis_index("gx"), lax.axis_index("gy")
    last_x, last_y = gx == gx_n - 1, gy == gy_n - 1

    loads = [
        pltpu.make_async_copy(sal.at[:, :, pl.ds(128 * j, 128)], u0.at[:, j], load_sem.at[j]) for j in range(2)
    ]
    loads.append(pltpu.make_async_copy(row_in.at[gx], row_v, load_sem.at[2]))
    loads.append(pltpu.make_async_copy(col_in.at[gy], col_v, load_sem.at[3]))
    for copy in loads:
        copy.start()

    barrier = pltpu.get_barrier_semaphore()
    x_peers = [(lax.rem(gx + k, gx_n), gy) for k in range(1, gx_n)]
    y_peers = [(gx, lax.rem(gy + k, gy_n)) for k in range(1, gy_n)]
    up, left = lax.rem(gx + gx_n - 1, gx_n), lax.rem(gy + gy_n - 1, gy_n)
    greeted = x_peers + y_peers + [(lax.rem(gx + 1, gx_n), lax.rem(gy + 1, gy_n))]
    for peer in greeted:
        pl.semaphore_signal(barrier, inc=1, device_id=peer, device_id_type=MESH)

    loads[0].wait()
    loads[1].wait()
    hrow[...] = jnp.concatenate([u0[:, 0, 0, :], u0[:, 1, 0, :]], axis=1)
    hcorner[...] = u0[:, 0, 0, :]
    lane = iota((n0, 128), 1)
    packed = jnp.zeros((n0, 128), jnp.float32)
    for d in range(DEPTH):
        packed = jnp.where(lane == d, u0[d, 0, :, 0:1], packed)
        packed = jnp.where(lane == 4 + d, u0[d, 1, :, 126:127], packed)
    packed = packed.T
    hcol[...] = packed[0:4]
    pl.semaphore_wait(barrier, len(greeted))
    halos = []
    for i, (src, dst, peer) in enumerate(
        ((hrow, hrow_in, (up, gy)), (hcol, hcol_in, (gx, left)), (hcorner, hcorner_in, (up, left)))
    ):
        copy = pltpu.make_async_remote_copy(
            src_ref=src, dst_ref=dst, send_sem=halo_send.at[i], recv_sem=halo_recv.at[i],
            device_id=peer, device_id_type=MESH,
        )
        copy.start()
        halos.append(copy)

    def send_all(peers, me, count, src, dst, send, recv):
        for k, peer in enumerate(peers):
            pltpu.make_async_remote_copy(
                src_ref=src.at[(me + k + 1) // count], dst_ref=dst.at[k], send_sem=send, recv_sem=recv,
                device_id=peer, device_id_type=MESH,
            ).start()

    def send_same(peers, src, dst, send, recv):
        for k, peer in enumerate(peers):
            pltpu.make_async_remote_copy(
                src_ref=src, dst_ref=dst.at[k + 1], send_sem=send, recv_sem=recv, device_id=peer, device_id_type=MESH
            ).start()

    def gather(buf, ref, places, count):
        at, _, _ = places["weight"]
        tiles = buf.shape[2] // 128
        sums = [jnp.zeros(buf.shape[1:], jnp.float32)] * 2
        for k in range(1, count):
            for way in range(2):
                weight = ref[at + way * count + k : at + way * count + k + 1, :]
                sums[way] = sums[way] + jnp.concatenate([weight] * tiles, axis=1) * buf[k - 1]
        return sums

    def selection(n, last):
        shape = (padded_lanes(n), padded_lanes(n // 2))
        row, lane = iota(shape, 0), iota(shape, 1)
        tail = jnp.where(last, n - 4, n)
        hit = ((lane < n // 2) & (row == 2 * lane)) | ((lane == n // 2) & (row == tail))
        return jnp.where(hit, 1.0, 0.0)

    def local_level(level, n, u, w):
        h = n // 2
        rows, rows_c, lanes_c = padded_rows(n), padded_rows(h), padded_lanes(h)
        col_mat, row_mat = col_table(f"mat{level}"), row_table(f"mat{level}")[:, 0:rows]
        select = selection(n, last_y)
        base, cols_local = [], jnp.zeros((8, rows_c), jnp.float32)
        row8, lane8 = iota((8, lanes_c), 0), iota((8, lanes_c), 1)
        is_tail = iota((rows_c, lanes_c), 0) == h
        for d in range(DEPTH):
            q = dot(w[d], col_mat)
            z = dot(row_mat, q)
            pick = ((row8 == d) & (lane8 == h + 1)) | ((row8 == 4 + d) & (lane8 == h + 2))
            cols_local += pick_dot(jnp.where(pick, 1.0, 0.0), z, 3, ((1,), (1,)), 0)
            even = even_rows(tall_v, pick_dot(u[d], select), rows_c)
            even = jnp.where(is_tail & last_x, even[h - 2 : h - 1, :], even)
            base.append(jnp.where(iota((rows_c, lanes_c), 1) <= h, z, 0.0) + even)
        tall = padded_lanes(h)
        if rows_c < tall:
            cols_local = jnp.concatenate([cols_local, jnp.zeros((8, tall - rows_c), jnp.float32)], axis=1)
        return base, cols_local

    def row_sums(values, weights, count=2):
        sums = []
        for way in range(count):
            for d in range(DEPTH):
                rows = values[d].shape[0]
                sums.append(jnp.sum(values[d] * weights[0:rows, way : way + 1], axis=0, keepdims=True))
        return jnp.concatenate(sums, axis=0)

    def line(value, functional):
        return jnp.sum(value * functional, axis=1, keepdims=True)

    def twice(table, row, lanes):
        return jnp.concatenate(
            [jnp.broadcast_to(table[row + way : row + way + 1, 0:lanes], (4, lanes)) for way in range(2)], axis=0
        )

    def outer(column, table, row, lanes):
        return (
            column[0:4] * table[row : row + 1, 0:lanes] + column[4:8] * table[row + 1 : row + 2, 0:lanes]
        )

    def spread_out(values, count, lanes, stride, pieces):
        mat = spread_matrix(count, lanes, stride, n0)
        for d in range(DEPTH):
            add_rows(out_v, d, pick_dot(values[d][0:count], mat, pieces), stride)

    n, h = n0, n0 // 2
    wide, rows_c, lanes_c = padded_lanes(n), padded_rows(h), padded_lanes(h)
    for copy in loads[2:]:
        copy.wait()
    rv, cv = row_table("vecs"), col_table("vecs")
    col_q = cv[0:2, 0:n]
    own_cols = jnp.zeros((n, 128), jnp.float32)
    for d in range(DEPTH):
        value = detail(jnp.concatenate([u0[d, 0], u0[d, 1]], axis=1), True)
        w0[d] = value
        for way in range(2):
            own_cols = jnp.where(lane == 4 * way + d, line(value, col_q[way : way + 1]), own_cols)
    own_rows = row_sums([w0[d] for d in range(DEPTH)], rv[0:8, 0:n].T)
    own_cols = own_cols.T[0:8]
    none = jnp.zeros((8, 128), jnp.float32)
    own_rows = jnp.concatenate([own_rows, none], axis=1)
    own_cols = jnp.concatenate([own_cols, none], axis=1)

    for copy in halos:
        copy.wait_recv()
    at = iota((4, wide), 1)
    own_254 = jnp.concatenate([u0[:, 0, n - 2, :], u0[:, 1, n - 2, :]], axis=1)
    next_row = jnp.where(last_x, own_254, hrow_in[...])
    next_col = jnp.where(last_y, packed[4:8], hcol_in[...])
    corner = jnp.where(
        last_y, next_row[:, n - 2 : n - 1], jnp.where(last_x, next_col[:, n - 2 : n - 1], hcorner_in[:, 0:1])
    )
    alias = packed[4:8, n - 2 : n - 1]
    wider = lambda value, end: jnp.where(at == n, end, jnp.concatenate([value, none[0:4]], axis=1))
    row_change, col_change = wider(next_row - own_254, 0.0), wider(next_col - packed[4:8], corner - alias)
    next_row, next_col = wider(next_row, alias), wider(next_col, corner)

    def between(value):
        mean = 0.5 * (pltpu.roll(value, 1, 1) + pltpu.roll(value, wide - 1, 1))
        return jnp.where(at > n, 0.0, jnp.where(at % 2 == 1, mean, value))

    row_255, row_256 = -0.5 * between(row_change), next_row - between(next_row)
    col_255, col_256 = -0.5 * between(col_change), next_col - between(next_col)
    for way in range(2):
        q = rv[way : way + 1, 0:wide]
        xs0[way] = (
            own_rows[4 * way : 4 * way + 4]
            + q[:, n - 1 : n] * row_255
            + q[:, n : n + 1] * row_256
            + jnp.where(at == n - 1, line(col_255, q), 0.0)
            + jnp.where(at == n, line(col_256, q), 0.0)
        )
    send_all(x_peers, gx, gx_n, xs0, xr0, x_send.at[0], x_recv.at[0])
    cols = []
    for way in range(2):
        q = cv[way : way + 1, 0:wide]
        cols.append(
            own_cols[4 * way : 4 * way + 4]
            + q[:, n - 1 : n] * col_255
            + q[:, n : n + 1] * col_256
            + jnp.where(at == n - 1, line(row_255, q), 0.0)
            + jnp.where(at == n, line(row_256, q), 0.0)
        )
    down_x = dot(jnp.concatenate(cols + [col_255, col_256], axis=0), row_table("mat0"), ((1,), (1,)))
    down_x = jnp.concatenate([down_x, jnp.zeros((16, lanes_c - rows_c), jnp.float32)], axis=1)
    select = selection(n, last_y)[0:n]
    next_even = pick_dot(next_row[:, 0:n], select)
    next_col_even = jnp.where(last_y, 0.0, pick_dot(next_col, selection(n, last_x)))
    evens = []
    for d in range(DEPTH):
        even = jnp.concatenate([u0[d, j, pl.ds(0, h, stride=2), :] for j in range(2)], axis=1)
        even = pick_dot(even, select)
        tail = jnp.where(last_x, even[h - 2 : h - 1], next_even[d : d + 1])
        tail = jnp.where(iota((8, lanes_c), 0) == 0, tail, 0.0)
        evens.append(jnp.concatenate([even, tail], axis=0))

    pltpu.make_async_copy(xr0, xr0, x_recv.at[0]).wait()
    a_right, a_left = gather(xr0, row_v, row_places, gx_n)
    q_r, q_l = cv[0:1, 0:wide], cv[1:2, 0:wide]
    p_r, p_l = rv[2:3, 0:lanes_c], rv[3:4, 0:lanes_c]
    ys0[0] = down_x[0:4] + line(a_right, q_r) * p_r + line(a_left, q_r) * p_l
    ys0[1] = down_x[4:8] + line(a_right, q_l) * p_r + line(a_left, q_l) * p_l
    send_all(y_peers, gy, gy_n, ys0, yr0, y_send.at[0], y_recv.at[0])
    col_mat, row_mat = col_table("mat0"), row_table("mat0")
    is_node = iota((1, lanes_c), 1) <= h
    base = []
    for d in range(DEPTH):
        z = dot(row_mat[:, 0:n], dot(w0[d], col_mat[0:n]))
        base.append(jnp.where(is_node, z, 0.0) + evens[d])
    down_turned = jnp.concatenate([col_255, col_255], axis=0).T[0:n]
    is_last = iota((n, 128), 1) == 127
    for d in range(DEPTH):
        out_v[d, 0] = w0[d, :, 0:128]
        out_v[d, 1] = w0[d, :, 128:256] + jnp.where(is_last, down_turned[:, d : d + 1], 0.0)
        for j in range(2):
            tail = iota((8, 128), 0) == 7
            fix = row_255[d : d + 1, 128 * j : 128 * j + 128]
            out_v[d, j, n - 8 : n, :] = out_v[d, j, n - 8 : n, :] + jnp.where(tail, fix, 0.0)
    carried = dot(jnp.concatenate([a_right, a_left, row_255, row_256], axis=0), col_mat)
    four = lambda row: jnp.broadcast_to(row, (4, lanes_c))
    other = jnp.concatenate(
        [jnp.where(is_node, carried, 0.0), twice(cv, 2, lanes_c)]
        + [four(jnp.where(is_node, col_mat[n - 1 + i : n + i, :], 0.0)) for i in range(2)]
        + [four(jnp.where(iota((1, lanes_c), 1) == h, 1.0, 0.0)), jnp.zeros((4, lanes_c), jnp.float32)],
        axis=0,
    )
    own = jnp.concatenate([twice(rv, 2, lanes_c), twice(rv, 4, lanes_c)], axis=0)
    rest = jnp.concatenate([down_x[8:16], next_col_even, jnp.zeros((4, lanes_c), jnp.float32)], axis=0)
    pltpu.make_async_copy(yr0, yr0, y_recv.at[0]).wait()
    c_right, c_left = gather(yr0, col_v, col_places, gy_n)
    lhs = jnp.concatenate([own, c_right, c_left, rest], axis=0).T[0:rows_c]
    for d in range(DEPTH):
        u1[d] = base[d] + dot(lhs, jnp.where(iota((40, lanes_c), 0) % 4 == d, other, 0.0))

    n, h, g = n0 // 2, n0 // 4, n0 // 8
    lane = iota((8, 128), 1)
    for d in range(DEPTH):
        w1[d] = detail(u1[d])
    ways = jnp.concatenate([rv[8:16, 0:256], row_table("taken")[:, 0:256]], axis=0).T
    functionals = jnp.concatenate([ways[:, 0:2], ways[:, 4:8]], axis=1)
    of_w = dot(row_sums([w1[d] for d in range(DEPTH)], functionals, 6), col_table("mat1"))
    taken = row_sums([u1[d] for d in range(DEPTH)], ways[:, 8:12], 4)
    of_next = of_w[8:24] + pick_dot(taken, selection(n, last_y))
    after = col_table("after")
    of_second = dot(jnp.concatenate([of_next[0:8], of_next[8:16]], axis=1), after[0:256])
    is_c = (lane == h + 1) | (lane == h + 2)
    sent = of_w[0:8] + pltpu.roll(of_second, h + 3, 1)
    for i in range(2):
        sent += pltpu.roll(jnp.where(is_c, of_w[8 + 8 * i : 16 + 8 * i], 0.0), g + 5 + 2 * i, 1)
    xs1[...] = sent
    xr1[0] = sent
    send_same(x_peers, xs1, xr1, x_send.at[1], x_recv.at[1])
    base1, cols1 = local_level(1, n, u1, w1)
    base2, cols2 = local_level(2, h, base1, [detail(base1[d]) for d in range(DEPTH)])
    others = xr1.at[pl.ds(1, gx_n - 1)]
    pltpu.make_async_copy(others, others, x_recv.at[1]).wait()
    got = dot(row_table("join")[:, 0 : gx_n * 8], xr1[...].reshape(gx_n * 8, 128))
    a_1 = got[0:8]
    a_2 = pltpu.roll(got[24:32], 128 - (h + 3), 1) + dot(
        jnp.concatenate([got[8:16], got[16:24]], axis=1), after[0:256]
    )
    msg, msg2, hs = [], [], []
    for way in range(2):
        msg.append(cols1[4 * way : 4 * way + 4] + outer(a_1[:, h + 1 + way : h + 2 + way], rv, 10, 128))
        row = outer(line(a_1, cv[16 + way : 17 + way, 0:128]), rv, 20, 128)
        row += outer(line(a_1, cv[12 + way : 13 + way, 0:128]), rv, 22, 128)
        row += outer(a_2[:, g + 1 + way : g + 2 + way], rv, 18, 128)
        msg2.append(cols2[4 * way : 4 * way + 4] + row)
        block = jnp.zeros((4, 128), jnp.float32)
        for i in range(2):
            at = h + g + 6 + 2 * i + way
            h_col = got[24:32, at : at + 1] + got[8 + 8 * i : 16 + 8 * i, h + 1 + way : h + 2 + way]
            for x_way in range(2):
                block += jnp.where(iota((4, 128), 1) == h + 1 + 2 * i + x_way, h_col[4 * x_way : 4 * x_way + 4], 0.0)
        hs.append(block)
    sent = jnp.concatenate(msg, axis=0) + pltpu.roll(jnp.concatenate(msg2, axis=0), h + 5, 1)
    sent += jnp.concatenate(hs, axis=0)
    ys1[...] = sent
    yr1[0] = sent
    send_same(y_peers, ys1, yr1, y_send.at[1], y_recv.at[1])
    spread_out([w1[d] for d in range(DEPTH)], n, 256, 2, 2)
    beside = lambda value: jnp.concatenate([value[128 * i : 128 * i + 128] for i in range(3)], axis=1)
    nodes_1 = lambda value: jnp.where(lane <= h, value, 0.0)
    nodes_2 = lambda value: jnp.where(lane <= g, value, 0.0)
    other1 = jnp.concatenate([nodes_1(a_1), twice(cv, 10, 128)], axis=0)
    across = dot(a_1, beside(after))
    other2 = jnp.concatenate(
        [nodes_2(across[:, 256:384]), nodes_2(across[:, 0:128]), nodes_2(across[:, 128:256]), nodes_2(a_2)]
        + [twice(cv, row, 128) for row in (24, 20, 22, 18)],
        axis=0,
    )
    own = jnp.concatenate([twice(rv, row, 128) for row in (24, 20, 22, 18)], axis=0)
    row_after = beside(row_table("after"))
    others = yr1.at[pl.ds(1, gy_n - 1)]
    pltpu.make_async_copy(others, others, y_recv.at[1]).wait()
    got = dot(col_table("join"), yr1[...].reshape(gy_n * 8, 128))
    down = dot(got[0:24], row_after)
    c_2 = nodes_2(pltpu.roll(got[24:32], 128 - (h + 5), 1) + down[8:16, 0:128] + down[16:24, 128:256])
    lhs = jnp.concatenate([own, down[0:8, 256:384], down[0:8, 0:128], down[0:8, 128:256], c_2], axis=0)
    lhs = jnp.concatenate([lhs, jnp.zeros_like(lhs)], axis=0).T[0 : padded_rows(g), 0:64]
    lhs1 = jnp.concatenate([twice(rv, 10, 128), nodes_1(got[0:8])], axis=0).T[0 : padded_rows(h)]
    details, last = [], []
    for d in range(DEPTH):
        last.append(base2[d] + dot(lhs, jnp.where(iota((64, 128), 0) % 4 == d, other2, 0.0)))
        nodes = base1[d] + dot(lhs1, jnp.where(iota((16, 128), 0) % 4 == d, other1, 0.0))
        details.append(detail(nodes))
    spread_out(details, h, 128, 4, 2)
    spread_out(last, g, 128, 8, 3)
    for d in range(DEPTH):
        out[d] = jnp.concatenate([out_v[d, j] for j in range(n0 // 128)], axis=1)

    for i, copy in enumerate(halos):
        copy.wait_send()
    pltpu.make_async_copy(xr0, xr0, x_send.at[0]).wait()
    pltpu.make_async_copy(yr0, yr0, y_send.at[0]).wait()
    others = xr1.at[pl.ds(1, gx_n - 1)]
    pltpu.make_async_copy(others, others, x_send.at[1]).wait()
    others = yr1.at[pl.ds(1, gy_n - 1)]
    pltpu.make_async_copy(others, others, y_send.at[1]).wait()


def even_rows(tall_v, value, rows_c):
    rows, lanes = value.shape
    half = rows // 2
    parts = []
    for j in range(lanes // 128):
        tall_v[j, 0:rows] = value[:, 128 * j : 128 * j + 128]
        part = tall_v[j, pl.ds(0, half, stride=2), :]
        parts.append(jnp.concatenate([part, jnp.zeros((rows_c - half, 128), jnp.float32)], axis=0))
    return jnp.concatenate(parts, axis=1)


def add_rows(ref, d, value, stride):
    place = pl.ds(0, value.shape[0], stride=stride)
    for j in range(ref.shape[1]):
        ref[d, j, place, :] = ref[d, j, place, :] + value[:, 128 * j : 128 * j + 128]


def shards(salinity):
    gx_n, gy_n = lax.axis_size("gx"), lax.axis_size("gy")
    _, nx, ny = salinity.shape
    n0 = nx
    (row_tab, row_places), (col_tab, col_places) = tables(nx * gx_n, ny * gy_n, gx_n, gy_n)
    vmem = lambda *shape: pltpu.VMEM(shape, jnp.float32)
    dma = lambda count: pltpu.SemaphoreType.DMA((count,))
    wide, wide_c = padded_lanes(n0), padded_lanes(n0 // 2)
    second = vmem(DEPTH, padded_rows(n0 // 2), padded_lanes(n0 // 2))
    scratch = [vmem(DEPTH, n0 // 128, n0, 128), vmem(DEPTH, 2, n0, 128), second, vmem(DEPTH, n0, n0), second, vmem(2, padded_rows(n0), 128)]
    scratch += [vmem(*row_tab.shape[1:]), vmem(*col_tab.shape[1:])]
    scratch += [vmem(DEPTH, n0), vmem(DEPTH, n0), vmem(DEPTH, 128)] * 2
    scratch += [vmem(2, DEPTH, wide), vmem(gx_n - 1, DEPTH, wide)]
    scratch += [vmem(2, DEPTH, wide_c), vmem(gy_n - 1, DEPTH, wide_c)]
    scratch += [vmem(8, 128), vmem(gx_n, 8, 128), vmem(8, 128), vmem(gy_n, 8, 128)]
    scratch += [dma(4), dma(3), dma(3), dma(2), dma(2), dma(2), dma(2)]
    anywhere = pl.BlockSpec(memory_space=pl.ANY)
    out = pl.pallas_call(
        functools.partial(kernel, gx_n, gy_n, n0, row_places, col_places),
        out_shape=jax.ShapeDtypeStruct(salinity.shape, jnp.float32),
        in_specs=[anywhere] * 3,
        out_specs=pl.BlockSpec(memory_space=pltpu.VMEM),
        scratch_shapes=scratch,
        compiler_params=pltpu.CompilerParams(
            collective_id=0, has_side_effects=True, vmem_limit_bytes=VMEM_LIMIT
        ),
    )(salinity, row_tab, col_tab)
    return out


def solution(mesh):
    placed = P(None, "gx", "gy")
    return jax.shard_map(shards, mesh=mesh, in_specs=(placed,), out_specs=placed, check_vma=False)
```

time: 50.4 us -> 39.8 us (0.79)
  Pallas kernels: 47.9 us -> 38.5 us
  local copies, waits for them, and re-layouts: 2.29 us -> 0.97 us
    pallas_call x1, Pallas kernels: 47.9 us -> 38.5 us  [shards(): pl.pallas_call(functools.partial(kernel, gx_n, gy_n, n0, row_places, col_...]
    unnamed x1, local copies, waits for them, and re-layouts: 2.29 us -> 0.97 us
where the time goes in v3:
time: 39.8 us; the launch traced here: 39.5 us
  Pallas kernels  38.5 us (97%)
  local copies, waits for them, and re-layouts  0.97 us (2%)
    pallas_call x1, Pallas kernels, shards(): pl.pallas_call(functools.partial(kernel, gx_n, gy_n, n0, row_places, col_...  38.5 us
    unnamed x1, local copies, waits for them, and re-layouts  0.97 us

profile of v3, /device:TPU:1, one launch (start us, length us, event | category | flops | bytes accessed | tf_op | source)
XLA Modules:
  0.0 39.5 jit_solution(11428647177500000903)
XLA Ops:
  0.0 38.5 %shard_map.37 = f32[4,256,256]{2,1,0:T(8,128)S(1)} custom-call(f32[4,256,256]{2,1,0:T(8,128)} %refs_0_.1, f32[8,1144,128]{2,1,0:T(8,128)} %constant.4.clone.refs_1_, f32[32,1760,128]{2,1,0:T(8,128)} %constant.5.clone.refs_2_), custom_call_target="tpu_custom_call" | custom-call | tf_op jit(solution)/shard_map/pallas_call | solution.py:617
  38.5 1.0 %copy.5 = f32[4,256,256]{2,1,0:T(8,128)} copy(f32[4,256,256]{2,1,0:T(8,128)S(1)} %shard_map.37) | data formatting | bytes 2097152

commit v4 on v3

--- a/solution.py
+++ b/solution.py
@@ -13,6 +13,7 @@
 LENGTH = 64.0
 MESH = pl.DeviceIdType.MESH
 TABLE_LANES = 384
+INNER = {8: 2, 32: 8}
 VMEM_LIMIT = 52 * 1024 * 1024
 
 
@@ -22,6 +23,20 @@
 
 def padded_lanes(count):
     return (count // 128 + 1) * 128 if count >= 128 else 128
+
+
+def partner(me, slot, tiles, sign):
+    inner = INNER.get(tiles, 1)
+    outer = tiles // inner
+    far = (me // inner + outer + sign * (slot // inner)) % outer
+    return far * inner + (me % inner + inner + sign * (slot % inner)) % inner
+
+
+def farthest_first(tiles):
+    inner = INNER.get(tiles, 1)
+    outer = tiles // inner
+    hops = lambda k: min(k // inner, outer - k // inner) + min(k % inner, inner - k % inner)
+    return sorted(range(1, tiles), key=lambda k: -hops(k))
 
 
 def solver_line(count):
@@ -90,7 +105,7 @@
         carry.append(np.stack([p[ids] / p[first], q[ids] / q_end]))
         weights = np.zeros((2, tiles))
         for k in range(1, tiles):
-            s = (t - k) % tiles
+            s = partner(t, k, tiles, -1)
             if s < t:
                 weights[0, k] = q[(s + 1) * h] * p[first] / w
             else:
@@ -123,7 +138,7 @@
     for t in range(tiles):
         for k in range(1, tiles):
             for way in range(2):
-                out[t, (t - k) % tiles, way, way] = weight[t, way, k]
+                out[t, partner(t, k, tiles, -1), way, way] = weight[t, way, k]
     return out
 
 
@@ -137,7 +152,7 @@
         for slot in range(tiles):
             for d in range(DEPTH):
                 for i, block in enumerate(blocks):
-                    out[t, i, :, d, slot, :, d] = block[t, (t - slot) % tiles]
+                    out[t, i, :, d, slot, :, d] = block[t, partner(t, slot, tiles, -1)]
     return out.reshape(tiles, 32, tiles * 8)
 
 
@@ -268,6 +283,14 @@
     gx, gy = lax.axis_index("gx"), lax.axis_index("gy")
     last_x, last_y = gx == gx_n - 1, gy == gy_n - 1
 
+    barrier = pltpu.get_barrier_semaphore()
+    x_peers = [(k, (partner(gx, k, gx_n, 1), gy)) for k in farthest_first(gx_n)]
+    y_peers = [(k, (gx, partner(gy, k, gy_n, 1))) for k in farthest_first(gy_n)]
+    up, left = lax.rem(gx + gx_n - 1, gx_n), lax.rem(gy + gy_n - 1, gy_n)
+    greeted = [peer for _, peer in y_peers + x_peers] + [(lax.rem(gx + 1, gx_n), lax.rem(gy + 1, gy_n))]
+    for peer in greeted:
+        pl.semaphore_signal(barrier, inc=1, device_id=peer, device_id_type=MESH)
+
     loads = [
         pltpu.make_async_copy(sal.at[:, :, pl.ds(128 * j, 128)], u0.at[:, j], load_sem.at[j]) for j in range(2)
     ]
@@ -276,14 +299,6 @@
     for copy in loads:
         copy.start()
 
-    barrier = pltpu.get_barrier_semaphore()
-    x_peers = [(lax.rem(gx + k, gx_n), gy) for k in range(1, gx_n)]
-    y_peers = [(gx, lax.rem(gy + k, gy_n)) for k in range(1, gy_n)]
-    up, left = lax.rem(gx + gx_n - 1, gx_n), lax.rem(gy + gy_n - 1, gy_n)
-    greeted = x_peers + y_peers + [(lax.rem(gx + 1, gx_n), lax.rem(gy + 1, gy_n))]
-    for peer in greeted:
-        pl.semaphore_signal(barrier, inc=1, device_id=peer, device_id_type=MESH)
-
     loads[0].wait()
     loads[1].wait()
     hrow[...] = jnp.concatenate([u0[:, 0, 0, :], u0[:, 1, 0, :]], axis=1)
@@ -295,29 +310,18 @@
         packed = jnp.where(lane == 4 + d, u0[d, 1, :, 126:127], packed)
     packed = packed.T
     hcol[...] = packed[0:4]
-    pl.semaphore_wait(barrier, len(greeted))
-    halos = []
-    for i, (src, dst, peer) in enumerate(
-        ((hrow, hrow_in, (up, gy)), (hcol, hcol_in, (gx, left)), (hcorner, hcorner_in, (up, left)))
-    ):
-        copy = pltpu.make_async_remote_copy(
-            src_ref=src, dst_ref=dst, send_sem=halo_send.at[i], recv_sem=halo_recv.at[i],
-            device_id=peer, device_id_type=MESH,
-        )
-        copy.start()
-        halos.append(copy)
-
-    def send_all(peers, me, count, src, dst, send, recv):
-        for k, peer in enumerate(peers):
+    def send_all(peers, axis, me, count, src, dst, send, recv):
+        for k, peer in peers:
+            way = (me + count - peer[axis]) // count
             pltpu.make_async_remote_copy(
-                src_ref=src.at[(me + k + 1) // count], dst_ref=dst.at[k], send_sem=send, recv_sem=recv,
+                src_ref=src.at[way], dst_ref=dst.at[k - 1], send_sem=send, recv_sem=recv,
                 device_id=peer, device_id_type=MESH,
             ).start()
 
     def send_same(peers, src, dst, send, recv):
-        for k, peer in enumerate(peers):
+        for k, peer in peers:
             pltpu.make_async_remote_copy(
-                src_ref=src, dst_ref=dst.at[k + 1], send_sem=send, recv_sem=recv, device_id=peer, device_id_type=MESH
+                src_ref=src, dst_ref=dst.at[k], send_sem=send, recv_sem=recv, device_id=peer, device_id_type=MESH
             ).start()
 
     def gather(buf, ref, places, count):
@@ -342,21 +346,15 @@
         rows, rows_c, lanes_c = padded_rows(n), padded_rows(h), padded_lanes(h)
         col_mat, row_mat = col_table(f"mat{level}"), row_table(f"mat{level}")[:, 0:rows]
         select = selection(n, last_y)
-        base, cols_local = [], jnp.zeros((8, rows_c), jnp.float32)
-        row8, lane8 = iota((8, lanes_c), 0), iota((8, lanes_c), 1)
+        base, solved = [], []
         is_tail = iota((rows_c, lanes_c), 0) == h
         for d in range(DEPTH):
-            q = dot(w[d], col_mat)
-            z = dot(row_mat, q)
-            pick = ((row8 == d) & (lane8 == h + 1)) | ((row8 == 4 + d) & (lane8 == h + 2))
-            cols_local += pick_dot(jnp.where(pick, 1.0, 0.0), z, 3, ((1,), (1,)), 0)
+            z = dot(row_mat, dot(w[d], col_mat))
             even = even_rows(tall_v, pick_dot(u[d], select), rows_c)
             even = jnp.where(is_tail & last_x, even[h - 2 : h - 1, :], even)
             base.append(jnp.where(iota((rows_c, lanes_c), 1) <= h, z, 0.0) + even)
-        tall = padded_lanes(h)
-        if rows_c < tall:
-            cols_local = jnp.concatenate([cols_local, jnp.zeros((8, tall - rows_c), jnp.float32)], axis=1)
-        return base, cols_local
+            solved.append(z)
+        return base, solved
 
     def row_sums(values, weights, count=2):
         sums = []
@@ -392,6 +390,18 @@
     col_q = cv[0:2, 0:n]
     own_cols = jnp.zeros((n, 128), jnp.float32)
     for d in range(DEPTH):
+        if d == DEPTH // 2:
+            pl.semaphore_wait(barrier, len(greeted))
+            halos = []
+            for i, (src, dst, peer) in enumerate(
+                ((hrow, hrow_in, (up, gy)), (hcol, hcol_in, (gx, left)), (hcorner, hcorner_in, (up, left)))
+            ):
+                copy = pltpu.make_async_remote_copy(
+                    src_ref=src, dst_ref=dst, send_sem=halo_send.at[i], recv_sem=halo_recv.at[i],
+                    device_id=peer, device_id_type=MESH,
+                )
+                copy.start()
+                halos.append(copy)
         value = detail(jnp.concatenate([u0[d, 0], u0[d, 1]], axis=1), True)
         w0[d] = value
         for way in range(2):
@@ -431,7 +441,7 @@
             + jnp.where(at == n - 1, line(col_255, q), 0.0)
             + jnp.where(at == n, line(col_256, q), 0.0)
         )
-    send_all(x_peers, gx, gx_n, xs0, xr0, x_send.at[0], x_recv.at[0])
+    send_all(x_peers, 0, gx, gx_n, xs0, xr0, x_send.at[0], x_recv.at[0])
     cols = []
     for way in range(2):
         q = cv[way : way + 1, 0:wide]
@@ -459,9 +469,12 @@
     a_right, a_left = gather(xr0, row_v, row_places, gx_n)
     q_r, q_l = cv[0:1, 0:wide], cv[1:2, 0:wide]
     p_r, p_l = rv[2:3, 0:lanes_c], rv[3:4, 0:lanes_c]
-    ys0[0] = down_x[0:4] + line(a_right, q_r) * p_r + line(a_left, q_r) * p_l
-    ys0[1] = down_x[4:8] + line(a_right, q_l) * p_r + line(a_left, q_l) * p_l
-    send_all(y_peers, gy, gy_n, ys0, yr0, y_send.at[0], y_recv.at[0])
+    layer = iota((4, 128), 0) == iota((4, 128), 1)
+    for way, q in enumerate((q_r, q_l)):
+        cols = down_x[4 * way : 4 * way + 4] + line(a_right, q) * p_r + line(a_left, q) * p_l
+        ys0[way, 0:4] = cols[:, 0:h]
+        ys0[way, 4:5] = jnp.sum(jnp.where(layer, cols[:, h : h + 1], 0.0), axis=0, keepdims=True)
+    send_all(y_peers, 1, gy, gy_n, ys0, yr0, y_send.at[0], y_recv.at[0])
     col_mat, row_mat = col_table("mat0"), row_table("mat0")
     is_node = iota((1, lanes_c), 1) <= h
     base = []
@@ -488,7 +501,11 @@
     own = jnp.concatenate([twice(rv, 2, lanes_c), twice(rv, 4, lanes_c)], axis=0)
     rest = jnp.concatenate([down_x[8:16], next_col_even, jnp.zeros((4, lanes_c), jnp.float32)], axis=0)
     pltpu.make_async_copy(yr0, yr0, y_recv.at[0]).wait()
-    c_right, c_left = gather(yr0, col_v, col_places, gy_n)
+    ends = []
+    for value in gather(yr0, col_v, col_places, gy_n):
+        tail = line(jnp.where(layer, jnp.broadcast_to(value[4:5], (4, 128)), 0.0), 1.0)
+        ends.append(jnp.concatenate([value[0:4], jnp.where(iota((4, 128), 1) == 0, tail, 0.0)], axis=1))
+    c_right, c_left = ends
     lhs = jnp.concatenate([own, c_right, c_left, rest], axis=0).T[0:rows_c]
     for d in range(DEPTH):
         u1[d] = base[d] + dot(lhs, jnp.where(iota((40, lanes_c), 0) % 4 == d, other, 0.0))
@@ -511,8 +528,17 @@
     xs1[...] = sent
     xr1[0] = sent
     send_same(x_peers, xs1, xr1, x_send.at[1], x_recv.at[1])
-    base1, cols1 = local_level(1, n, u1, w1)
-    base2, cols2 = local_level(2, h, base1, [detail(base1[d]) for d in range(DEPTH)])
+    base1, solved1 = local_level(1, n, u1, w1)
+    cols = jnp.zeros((padded_rows(h), 128), jnp.float32)
+    spot = iota(cols.shape, 1)
+    for d in range(DEPTH):
+        for way in range(2):
+            cols = jnp.where(spot == 4 * way + d, solved1[d][:, h + 1 + way : h + 2 + way], cols)
+            cols = jnp.where(spot == 8 + 4 * way + d, line(base1[d], cv[16 + way : 17 + way, 0:128]), cols)
+            cols = jnp.where(spot == 16 + 4 * way + d, line(base1[d], cv[12 + way : 13 + way, 0:128]), cols)
+    cols = jnp.concatenate([cols, jnp.zeros((128 - padded_rows(h), 128), jnp.float32)], axis=0).T
+    row_after = row_table("after")
+    cols1, cols2 = cols[0:8], dot(jnp.concatenate([cols[8:16], cols[16:24]], axis=1), row_after[0:256])
     others = xr1.at[pl.ds(1, gx_n - 1)]
     pltpu.make_async_copy(others, others, x_recv.at[1]).wait()
     got = dot(row_table("join")[:, 0 : gx_n * 8], xr1[...].reshape(gx_n * 8, 128))
@@ -539,6 +565,7 @@
     ys1[...] = sent
     yr1[0] = sent
     send_same(y_peers, ys1, yr1, y_send.at[1], y_recv.at[1])
+    base2, _ = local_level(2, h, base1, [detail(base1[d]) for d in range(DEPTH)])
     spread_out([w1[d] for d in range(DEPTH)], n, 256, 2, 2)
     beside = lambda value: jnp.concatenate([value[128 * i : 128 * i + 128] for i in range(3)], axis=1)
     nodes_1 = lambda value: jnp.where(lane <= h, value, 0.0)
@@ -551,7 +578,7 @@
         axis=0,
     )
     own = jnp.concatenate([twice(rv, row, 128) for row in (24, 20, 22, 18)], axis=0)
-    row_after = beside(row_table("after"))
+    row_after = beside(row_after)
     others = yr1.at[pl.ds(1, gy_n - 1)]
     pltpu.make_async_copy(others, others, y_recv.at[1]).wait()
     got = dot(col_table("join"), yr1[...].reshape(gy_n * 8, 128))
@@ -604,13 +631,13 @@
     (row_tab, row_places), (col_tab, col_places) = tables(nx * gx_n, ny * gy_n, gx_n, gy_n)
     vmem = lambda *shape: pltpu.VMEM(shape, jnp.float32)
     dma = lambda count: pltpu.SemaphoreType.DMA((count,))
-    wide, wide_c = padded_lanes(n0), padded_lanes(n0 // 2)
+    wide = padded_lanes(n0)
     second = vmem(DEPTH, padded_rows(n0 // 2), padded_lanes(n0 // 2))
     scratch = [vmem(DEPTH, n0 // 128, n0, 128), vmem(DEPTH, 2, n0, 128), second, vmem(DEPTH, n0, n0), second, vmem(2, padded_rows(n0), 128)]
     scratch += [vmem(*row_tab.shape[1:]), vmem(*col_tab.shape[1:])]
     scratch += [vmem(DEPTH, n0), vmem(DEPTH, n0), vmem(DEPTH, 128)] * 2
     scratch += [vmem(2, DEPTH, wide), vmem(gx_n - 1, DEPTH, wide)]
-    scratch += [vmem(2, DEPTH, wide_c), vmem(gy_n - 1, DEPTH, wide_c)]
+    scratch += [vmem(2, DEPTH + 1, n0 // 2), vmem(gy_n - 1, DEPTH + 1, n0 // 2)]
     scratch += [vmem(8, 128), vmem(gx_n, 8, 128), vmem(8, 128), vmem(gy_n, 8, 128)]
     scratch += [dma(4), dma(3), dma(3), dma(2), dma(2), dma(2), dma(2)]
     anywhere = pl.BlockSpec(memory_space=pl.ANY)

time: 39.8 us -> 37.8 us (0.950)
  Pallas kernels: 38.5 us -> 36.7 us
    pallas_call x1, Pallas kernels: 38.5 us -> 36.7 us  [shards(): pl.pallas_call(functools.partial(kernel, gx_n, gy_n, n0, row_places, col_...]
where the time goes in v4:
time: 37.8 us; the launch traced here: 37.7 us
  Pallas kernels  36.7 us (97%)
  local copies, waits for them, and re-layouts  0.97 us (3%)
    pallas_call x1, Pallas kernels, shards(): pl.pallas_call(functools.partial(kernel, gx_n, gy_n, n0, row_places, col_...  36.7 us
    unnamed x1, local copies, waits for them, and re-layouts  0.97 us

profile of v4, /device:TPU:1, one launch (start us, length us, event | category | flops | bytes accessed | tf_op | source)
XLA Modules:
  0.0 37.7 jit_solution(12133245743192595787)
XLA Ops:
  0.0 36.7 %shard_map.37 = f32[4,256,256]{2,1,0:T(8,128)S(1)} custom-call(f32[4,256,256]{2,1,0:T(8,128)} %refs_0_.1, f32[8,1144,128]{2,1,0:T(8,128)} %constant.4.clone.refs_1_, f32[32,1760,128]{2,1,0:T(8,128)} %constant.5.clone.refs_2_), custom_call_target="tpu_custom_call" | custom-call | tf_op jit(solution)/shard_map/pallas_call | solution.py:644
  36.8 1.0 %copy.5 = f32[4,256,256]{2,1,0:T(8,128)} copy(f32[4,256,256]{2,1,0:T(8,128)S(1)} %shard_map.37) | data formatting | bytes 2097152

commit v5 on v4

--- a/solution.py
+++ b/solution.py
@@ -81,7 +81,7 @@
     h = n // 2
     coarse = total // 2
     q, p, w = solver_line(coarse)
-    local, functional, carry, weight, select = [], [], [], [], []
+    local, functional, carry, weight, select, wide = [], [], [], [], [], []
     for t in range(tiles):
         first = t * h
         last_tile = t == tiles - 1
@@ -99,6 +99,10 @@
         q_end = q[min(first + h, coarse - 1)]
         to_right = (np.where(inside, q[safe] / q_end, 0.0)) @ load
         to_left = (np.where(inside, p[safe] / p[first], 0.0)) @ load
+        before = load_block(total, window, np.array([t * n - 1]))
+        own = [np.append(f[:n], np.where(inside, v, 0.0) @ before) for f, v in
+               ((to_right, q[safe] / q_end), (to_left, p[safe] / p[first]))]
+        wide.append(np.stack(own + [own[0] * q_end * p[first] / w]))
         to_right[n] = 0.0
         to_left[0] = 0.0
         functional.append(np.stack([to_right, to_left]))
@@ -115,7 +119,7 @@
         pick[2 * np.arange(h), np.arange(h)] = 1.0
         pick[n - 4 if last_tile else n, h] = 1.0
         select.append(pick)
-    return [np.stack(item) for item in (local, functional, carry, weight, select)]
+    return [np.stack(item) for item in (local, functional, carry, weight, select, wide)]
 
 
 def fit(array, shape):
@@ -175,11 +179,14 @@
     for vecs, size, tiles, out in ((row_vecs, nx, gx, row_out), (col_vecs, ny, gy, col_out)):
         lines = [line_tables(size >> level, tiles) for level in range(LEVELS)]
         sides.append(lines)
-        for level, (local, functional, carry, weight, select) in enumerate(lines):
+        for level, (local, functional, carry, weight, select, wide) in enumerate(lines):
             n = (size >> level) // tiles
             h = n // 2
             vecs[:, 8 * level : 8 * level + 2, : n + 1] = functional
             vecs[:, 8 * level + 2 : 8 * level + 4, : h + 1] = carry
+            if level == 0:
+                vecs[:, 26:29, :n] = wide[:, :, :n]
+                vecs[:, 26:29, n + 1] = wide[:, :, n]
             if vecs is row_vecs:
                 out[f"mat{level}"] = fit(local, (padded_rows(h), padded_lanes(n)))
                 if level == 0:
@@ -192,7 +199,7 @@
     nodes = (nx // gx >> 2) + 1
     inter = interpolation(nodes)
     rest = np.eye(nodes) - inter
-    (local_a, _, carry_a, weight_a, select_a), (local_b, func_b, carry_b, weight_b, select_b) = sides[0][1:]
+    (local_a, _, carry_a, weight_a, select_a, _), (local_b, func_b, carry_b, weight_b, select_b, _) = sides[0][1:]
     row_k = [np.einsum("tbi,ij,taj->tba", func_b, op, carry_a) for op in (rest, inter)]
     row_out["join"] = joined_weights(pair_weights(weight_a), row_k, pair_weights(weight_b))
     after = np.zeros((gx, 384, 128))
@@ -208,7 +215,7 @@
     after[:, 256 : 256 + nodes, :half] = select_b
     row_vecs[:, 24:26, :half] = carry_a @ select_b
     row_out.update(after=after, taken=taken, vecs=row_vecs)
-    (_, _, carry_a, weight_a, _), (local_b, func_b, _, weight_b, select_b) = sides[1][1:]
+    (_, _, carry_a, weight_a, _, _), (local_b, func_b, _, weight_b, select_b, _) = sides[1][1:]
     col_k = [np.einsum("tbi,ij,taj->tba", func_b, op, carry_a) for op in (np.eye(nodes), rest)]
     col_out["join"] = joined_weights(pair_weights(weight_a), col_k, pair_weights(weight_b))
     after = np.zeros((gy, 384, 128))
@@ -312,7 +319,8 @@
     hcol[...] = packed[0:4]
     def send_all(peers, axis, me, count, src, dst, send, recv):
         for k, peer in peers:
-            way = (me + count - peer[axis]) // count
+            before = (me + count - 1 - peer[axis]) // count
+            way = before + before * (1 - (me + count - 2 - peer[axis]) // count)
             pltpu.make_async_remote_copy(
                 src_ref=src.at[way], dst_ref=dst.at[k - 1], send_sem=send, recv_sem=recv,
                 device_id=peer, device_id_type=MESH,
@@ -390,58 +398,74 @@
     col_q = cv[0:2, 0:n]
     own_cols = jnp.zeros((n, 128), jnp.float32)
     for d in range(DEPTH):
-        if d == DEPTH // 2:
-            pl.semaphore_wait(barrier, len(greeted))
-            halos = []
-            for i, (src, dst, peer) in enumerate(
-                ((hrow, hrow_in, (up, gy)), (hcol, hcol_in, (gx, left)), (hcorner, hcorner_in, (up, left)))
-            ):
-                copy = pltpu.make_async_remote_copy(
-                    src_ref=src, dst_ref=dst, send_sem=halo_send.at[i], recv_sem=halo_recv.at[i],
-                    device_id=peer, device_id_type=MESH,
-                )
-                copy.start()
-                halos.append(copy)
         value = detail(jnp.concatenate([u0[d, 0], u0[d, 1]], axis=1), True)
         w0[d] = value
         for way in range(2):
             own_cols = jnp.where(lane == 4 * way + d, line(value, col_q[way : way + 1]), own_cols)
-    own_rows = row_sums([w0[d] for d in range(DEPTH)], rv[0:8, 0:n].T)
+    own_rows = row_sums([w0[d] for d in range(DEPTH)], rv[24:32, 0:n].T[:, 2:4])
     own_cols = own_cols.T[0:8]
     none = jnp.zeros((8, 128), jnp.float32)
     own_rows = jnp.concatenate([own_rows, none], axis=1)
     own_cols = jnp.concatenate([own_cols, none], axis=1)
-
-    for copy in halos:
-        copy.wait_recv()
     at = iota((4, wide), 1)
     own_254 = jnp.concatenate([u0[:, 0, n - 2, :], u0[:, 1, n - 2, :]], axis=1)
-    next_row = jnp.where(last_x, own_254, hrow_in[...])
-    next_col = jnp.where(last_y, packed[4:8], hcol_in[...])
-    corner = jnp.where(
-        last_y, next_row[:, n - 2 : n - 1], jnp.where(last_x, next_col[:, n - 2 : n - 1], hcorner_in[:, 0:1])
-    )
     alias = packed[4:8, n - 2 : n - 1]
     wider = lambda value, end: jnp.where(at == n, end, jnp.concatenate([value, none[0:4]], axis=1))
-    row_change, col_change = wider(next_row - own_254, 0.0), wider(next_col - packed[4:8], corner - alias)
-    next_row, next_col = wider(next_row, alias), wider(next_col, corner)
 
     def between(value):
         mean = 0.5 * (pltpu.roll(value, 1, 1) + pltpu.roll(value, wide - 1, 1))
         return jnp.where(at > n, 0.0, jnp.where(at % 2 == 1, mean, value))
 
-    row_255, row_256 = -0.5 * between(row_change), next_row - between(next_row)
-    col_255, col_256 = -0.5 * between(col_change), next_col - between(next_col)
+    def edges(next_row, next_col, corner):
+        corner = jnp.where(
+            last_y, next_row[:, n - 2 : n - 1], jnp.where(last_x, next_col[:, n - 2 : n - 1], corner)
+        )
+        row_change, col_change = wider(next_row - own_254, 0.0), wider(next_col - packed[4:8], corner - alias)
+        next_row, next_col = wider(next_row, alias), wider(next_col, corner)
+        rows = -0.5 * between(row_change), next_row - between(next_row)
+        cols = -0.5 * between(col_change), next_col - between(next_col)
+        return rows + cols + (next_row, next_col)
+
+    zero_row = jnp.where(last_x, own_254, 0.0)
+    zero_col = jnp.where(last_y, packed[4:8], 0.0)
+    end_row, _, end_col, _, _, _ = edges(zero_row, zero_col, 0.0)
+    first_row, first_col = hrow[...], hcol[...]
+    prior_row = -0.5 * between(wider(first_row, jnp.where(last_y, first_row[:, n - 2 : n - 1], 0.0)))
+    prior_row = jnp.where(at == n, 0.0, prior_row)
+    prior_col = -0.5 * between(wider(first_col, jnp.where(last_x, first_col[:, n - 2 : n - 1], 0.0)))
+    prior_col = jnp.where(at == n, 0.0, prior_col)
+    prior_row = jnp.where(at == n + 1, -0.25 * first_row[:, 0:1], prior_row)
+    row_0 = jnp.concatenate([w0[:, 0, :], none[0:4]], axis=1)
     for way in range(2):
-        q = rv[way : way + 1, 0:wide]
-        xs0[way] = (
-            own_rows[4 * way : 4 * way + 4]
-            + q[:, n - 1 : n] * row_255
-            + q[:, n : n + 1] * row_256
-            + jnp.where(at == n - 1, line(col_255, q), 0.0)
-            + jnp.where(at == n, line(col_256, q), 0.0)
+        q = rv[26 + way : 27 + way, 0:wide]
+        q_own = jnp.where(iota((1, wide), 1) < n, q, 0.0)
+        message = own_rows[4 * way : 4 * way + 4] + q[:, n - 1 : n] * end_row
+        message += jnp.where(at == n - 1, line(end_col, q_own), 0.0)
+        message += jnp.where(at == n + 1, line(prior_col, q_own), 0.0)
+        message = jnp.where(at == n, 0.0, message)
+        xs0[way] = message + q[:, n + 1 : n + 2] * prior_row
+        if way == 1:
+            message -= q[:, 0:1] * row_0
+            message -= jnp.where(at == n - 1, q[:, 0:1] * end_col[:, 0:1], 0.0)
+            message -= jnp.where(at == n + 1, q[:, 0:1] * prior_col[:, 0:1], 0.0)
+            xs0[2] = message
+    pl.semaphore_wait(barrier, len(greeted))
+    send_all(x_peers, 0, gx, gx_n, xs0, xr0, x_send.at[0], x_recv.at[0])
+    halos = []
+    for i, (src, dst, peer) in enumerate(
+        ((hrow, hrow_in, (up, gy)), (hcol, hcol_in, (gx, left)), (hcorner, hcorner_in, (up, left)))
+    ):
+        copy = pltpu.make_async_remote_copy(
+            src_ref=src, dst_ref=dst, send_sem=halo_send.at[i], recv_sem=halo_recv.at[i],
+            device_id=peer, device_id_type=MESH,
         )
-    send_all(x_peers, 0, gx, gx_n, xs0, xr0, x_send.at[0], x_recv.at[0])
+        copy.start()
+        halos.append(copy)
+    for copy in halos:
+        copy.wait_recv()
+    row_255, row_256, col_255, col_256, next_row, next_col = edges(
+        jnp.where(last_x, own_254, hrow_in[...]), jnp.where(last_y, packed[4:8], hcol_in[...]), hcorner_in[:, 0:1]
+    )
     cols = []
     for way in range(2):
         q = cv[way : way + 1, 0:wide]
@@ -467,13 +491,20 @@
 
     pltpu.make_async_copy(xr0, xr0, x_recv.at[0]).wait()
     a_right, a_left = gather(xr0, row_v, row_places, gx_n)
-    q_r, q_l = cv[0:1, 0:wide], cv[1:2, 0:wide]
+    a_right += rv[28:29, n + 1 : n + 2] * prior_row
     p_r, p_l = rv[2:3, 0:lanes_c], rv[3:4, 0:lanes_c]
-    layer = iota((4, 128), 0) == iota((4, 128), 1)
-    for way, q in enumerate((q_r, q_l)):
+    lane4 = iota((4, 128), 1)
+    layer = iota((4, 128), 0)
+    shared = jnp.zeros((4, 128), jnp.float32)
+    for i, value in enumerate((a_right[:, n + 1 : n + 2], a_left[:, n + 1 : n + 2], a_right[:, 0:1], a_left[:, 0:1])):
+        shared = jnp.where(lane4 == 4 * (i + 1) + layer, value, shared)
+    q_right, q_left = cv[26:27, 0:wide], cv[27:28, 0:wide]
+    q_near = jnp.where((iota((1, wide), 1) == 0) | (iota((1, wide), 1) == n + 1), 0.0, q_left)
+    for i, q in enumerate((q_right, q_left, q_near)):
+        way = (i + 1) // 2
         cols = down_x[4 * way : 4 * way + 4] + line(a_right, q) * p_r + line(a_left, q) * p_l
-        ys0[way, 0:4] = cols[:, 0:h]
-        ys0[way, 4:5] = jnp.sum(jnp.where(layer, cols[:, h : h + 1], 0.0), axis=0, keepdims=True)
+        ys0[i, 0:4] = cols[:, 0:h]
+        ys0[i, 4:5] = jnp.sum(jnp.where(lane4 == layer, cols[:, h : h + 1], shared), axis=0, keepdims=True)
     send_all(y_peers, 1, gy, gy_n, ys0, yr0, y_send.at[0], y_recv.at[0])
     col_mat, row_mat = col_table("mat0"), row_table("mat0")
     is_node = iota((1, lanes_c), 1) <= h
@@ -503,9 +534,17 @@
     pltpu.make_async_copy(yr0, yr0, y_recv.at[0]).wait()
     ends = []
     for value in gather(yr0, col_v, col_places, gy_n):
-        tail = line(jnp.where(layer, jnp.broadcast_to(value[4:5], (4, 128)), 0.0), 1.0)
+        tail = line(jnp.where(lane4 == layer, jnp.broadcast_to(value[4:5], (4, 128)), 0.0), 1.0)
         ends.append(jnp.concatenate([value[0:4], jnp.where(iota((4, 128), 1) == 0, tail, 0.0)], axis=1))
     c_right, c_left = ends
+    c_right += cv[28:29, n + 1 : n + 2] * (a_right[:, n + 1 : n + 2] * p_r + a_left[:, n + 1 : n + 2] * p_l)
+    inner = INNER.get(gy_n, 1)
+    near = inner - 1 + (gy_n - inner) * ((gy % inner + 1) // inner)
+    told = jnp.where(last_y, 0.0, jnp.broadcast_to(yr0[near - 1, 4:5, :], (4, 128)))
+    told = [line(jnp.where(lane4 == 4 * (i + 1) + layer, told, 0.0), 1.0) for i in range(4)]
+    ends_y = [jnp.where(is_node, col_mat[n - 1 + i : n + i, :], 0.0) for i in range(2)]
+    late = jnp.concatenate([told[i] * ends_y[0] + told[2 + i] * ends_y[1] for i in range(2)], axis=0)
+    other = other + jnp.concatenate([late, jnp.zeros((32, lanes_c), jnp.float32)], axis=0)
     lhs = jnp.concatenate([own, c_right, c_left, rest], axis=0).T[0:rows_c]
     for d in range(DEPTH):
         u1[d] = base[d] + dot(lhs, jnp.where(iota((40, lanes_c), 0) % 4 == d, other, 0.0))
@@ -636,8 +675,8 @@
     scratch = [vmem(DEPTH, n0 // 128, n0, 128), vmem(DEPTH, 2, n0, 128), second, vmem(DEPTH, n0, n0), second, vmem(2, padded_rows(n0), 128)]
     scratch += [vmem(*row_tab.shape[1:]), vmem(*col_tab.shape[1:])]
     scratch += [vmem(DEPTH, n0), vmem(DEPTH, n0), vmem(DEPTH, 128)] * 2
-    scratch += [vmem(2, DEPTH, wide), vmem(gx_n - 1, DEPTH, wide)]
-    scratch += [vmem(2, DEPTH + 1, n0 // 2), vmem(gy_n - 1, DEPTH + 1, n0 // 2)]
+    scratch += [vmem(3, DEPTH, wide), vmem(gx_n - 1, DEPTH, wide)]
+    scratch += [vmem(3, DEPTH + 1, n0 // 2), vmem(gy_n - 1, DEPTH + 1, n0 // 2)]
     scratch += [vmem(8, 128), vmem(gx_n, 8, 128), vmem(8, 128), vmem(gy_n, 8, 128)]
     scratch += [dma(4), dma(3), dma(3), dma(2), dma(2), dma(2), dma(2)]
     anywhere = pl.BlockSpec(memory_space=pl.ANY)

time: 37.8 us -> 35.5 us (0.939)
  Pallas kernels: 36.7 us -> 34.4 us
    pallas_call x1, Pallas kernels: 36.7 us -> 34.4 us  [shards(): pl.pallas_call(functools.partial(kernel, gx_n, gy_n, n0, row_places, col_...]
where the time goes in v5:
time: 35.5 us; the launch traced here: 35.4 us
  Pallas kernels  34.4 us (97%)
  local copies, waits for them, and re-layouts  0.97 us (3%)
    pallas_call x1, Pallas kernels, shards(): pl.pallas_call(functools.partial(kernel, gx_n, gy_n, n0, row_places, col_...  34.4 us
    unnamed x1, local copies, waits for them, and re-layouts  0.97 us

profile of v5, /device:TPU:1, one launch (start us, length us, event | category | flops | bytes accessed | tf_op | source)
XLA Modules:
  0.0 35.4 jit_solution(10219978549116443584)
XLA Ops:
  0.0 34.4 %shard_map.37 = f32[4,256,256]{2,1,0:T(8,128)S(1)} custom-call(f32[4,256,256]{2,1,0:T(8,128)} %refs_0_.1, f32[8,1144,128]{2,1,0:T(8,128)} %constant.4.clone.refs_1_, f32[32,1760,128]{2,1,0:T(8,128)} %constant.5.clone.refs_2_), custom_call_target="tpu_custom_call" | custom-call | tf_op jit(solution)/shard_map/pallas_call | solution.py:683
  34.4 1.0 %copy.5 = f32[4,256,256]{2,1,0:T(8,128)} copy(f32[4,256,256]{2,1,0:T(8,128)S(1)} %shard_map.37) | data formatting | bytes 2097152

commit v6 on v5

--- a/solution.py
+++ b/solution.py
@@ -13,6 +13,7 @@
 LENGTH = 64.0
 MESH = pl.DeviceIdType.MESH
 TABLE_LANES = 384
+BEFORE_HALO = 2
 INNER = {8: 2, 32: 8}
 VMEM_LIMIT = 52 * 1024 * 1024
 
@@ -214,7 +215,17 @@
         after[:, 128 * i + nodes + 2 * i : 128 * i + nodes + 2 * i + 2, :half] = carry_b
     after[:, 256 : 256 + nodes, :half] = select_b
     row_vecs[:, 24:26, :half] = carry_a @ select_b
-    row_out.update(after=after, taken=taken, vecs=row_vecs)
+    fine = local_a.shape[2]
+    inter_a = interpolation(fine)
+    rest_a = np.eye(fine) - inter_a
+    of_w = [sides[0][1][1], row_vecs[:, 12:14, :fine], row_vecs[:, 14:16, :fine]]
+    late = [of_w[0] @ rest_a, of_w[0] @ inter_a]
+    for i in range(2):
+        late += [of_w[1 + i] @ rest_a, of_w[1 + i] @ inter_a, taken[:, 2 * i : 2 * i + 2, :fine]]
+    late = np.stack(late, axis=1)
+    late_own = np.einsum("tmxi,tpi->txpm", late, sides[0][0][2]).reshape(gx, 4, 8)
+    late = late.reshape(gx, 16, fine).transpose(0, 2, 1)
+    row_out.update(after=after, taken=taken, vecs=row_vecs, late=fit(late, (256, 128)), late_own=fit(late_own, (8, 128)))
     (_, _, carry_a, weight_a, _, _), (local_b, func_b, _, weight_b, select_b, _) = sides[1][1:]
     col_k = [np.einsum("tbi,ij,taj->tba", func_b, op, carry_a) for op in (np.eye(nodes), rest)]
     col_out["join"] = joined_weights(pair_weights(weight_a), col_k, pair_weights(weight_b))
@@ -226,7 +237,24 @@
         after[:, 128 * i : 128 * i + nodes, : both.shape[1]] = (both @ op).transpose(0, 2, 1)
     after[:, 256 : 256 + nodes, :half] = select_b
     col_vecs[:, 24:26, :half] = carry_a @ select_b
-    col_out.update(after=after, vecs=col_vecs)
+    first = np.concatenate(sides[1][1][0:2], axis=1)
+    select_a = sides[1][1][4]
+    vectors = [sides[1][0][2][:, 0], sides[1][0][2][:, 1], sides[1][0][0][:, :, -2], sides[1][0][0][:, :, -1]]
+    late = np.zeros((gy, 4, 8, 128))
+    lanes = first.shape[1]
+    for i, vector in enumerate(vectors):
+        for t in range(gy):
+            for k, op in enumerate((np.eye(fine), rest_a)):
+                image = first[t] @ (op @ vector[t])
+                late[t, i, k, :lanes] = image
+                for m, second in enumerate((np.eye(nodes), rest)):
+                    at = 2 + 3 * m + k
+                    late[t, i, at, lanes : lanes + both.shape[1]] = both[t] @ (second @ image[:nodes])
+                    start = lanes + both.shape[1] + 2 * m
+                    late[t, i, at, start : start + 2] = image[nodes:lanes]
+            for m, second in enumerate((np.eye(nodes), rest)):
+                late[t, i, 4 + 3 * m, lanes : lanes + both.shape[1]] = both[t] @ (second @ (vector[t] @ select_a[t]))
+    col_out.update(after=after, vecs=col_vecs, late=late.reshape(gy, 32, 128))
     return packed(row_out), packed(col_out)
 
 
@@ -461,6 +489,15 @@
         )
         copy.start()
         halos.append(copy)
+    col_mat, row_mat = col_table("mat0"), row_table("mat0")
+    is_node = iota((1, lanes_c), 1) <= h
+
+    def dense(layers):
+        half = jnp.concatenate([dot(row_mat[:, 0:n0], w0[d]) for d in layers], axis=0)
+        value = jnp.where(is_node, dot(half, col_mat[0:n0]), 0.0)
+        return [value[i * rows_c : (i + 1) * rows_c] for i in range(len(layers))]
+
+    base = dense(range(BEFORE_HALO))
     for copy in halos:
         copy.wait_recv()
     row_255, row_256, col_255, col_256, next_row, next_col = edges(
@@ -506,21 +543,8 @@
         ys0[i, 0:4] = cols[:, 0:h]
         ys0[i, 4:5] = jnp.sum(jnp.where(lane4 == layer, cols[:, h : h + 1], shared), axis=0, keepdims=True)
     send_all(y_peers, 1, gy, gy_n, ys0, yr0, y_send.at[0], y_recv.at[0])
-    col_mat, row_mat = col_table("mat0"), row_table("mat0")
-    is_node = iota((1, lanes_c), 1) <= h
-    base = []
-    for d in range(DEPTH):
-        z = dot(row_mat[:, 0:n], dot(w0[d], col_mat[0:n]))
-        base.append(jnp.where(is_node, z, 0.0) + evens[d])
-    down_turned = jnp.concatenate([col_255, col_255], axis=0).T[0:n]
-    is_last = iota((n, 128), 1) == 127
-    for d in range(DEPTH):
-        out_v[d, 0] = w0[d, :, 0:128]
-        out_v[d, 1] = w0[d, :, 128:256] + jnp.where(is_last, down_turned[:, d : d + 1], 0.0)
-        for j in range(2):
-            tail = iota((8, 128), 0) == 7
-            fix = row_255[d : d + 1, 128 * j : 128 * j + 128]
-            out_v[d, j, n - 8 : n, :] = out_v[d, j, n - 8 : n, :] + jnp.where(tail, fix, 0.0)
+    base += dense(range(BEFORE_HALO, DEPTH))
+    base = [base[d] + evens[d] for d in range(DEPTH)]
     carried = dot(jnp.concatenate([a_right, a_left, row_255, row_256], axis=0), col_mat)
     four = lambda row: jnp.broadcast_to(row, (4, lanes_c))
     other = jnp.concatenate(
@@ -531,28 +555,13 @@
     )
     own = jnp.concatenate([twice(rv, 2, lanes_c), twice(rv, 4, lanes_c)], axis=0)
     rest = jnp.concatenate([down_x[8:16], next_col_even, jnp.zeros((4, lanes_c), jnp.float32)], axis=0)
-    pltpu.make_async_copy(yr0, yr0, y_recv.at[0]).wait()
-    ends = []
-    for value in gather(yr0, col_v, col_places, gy_n):
-        tail = line(jnp.where(lane4 == layer, jnp.broadcast_to(value[4:5], (4, 128)), 0.0), 1.0)
-        ends.append(jnp.concatenate([value[0:4], jnp.where(iota((4, 128), 1) == 0, tail, 0.0)], axis=1))
-    c_right, c_left = ends
-    c_right += cv[28:29, n + 1 : n + 2] * (a_right[:, n + 1 : n + 2] * p_r + a_left[:, n + 1 : n + 2] * p_l)
-    inner = INNER.get(gy_n, 1)
-    near = inner - 1 + (gy_n - inner) * ((gy % inner + 1) // inner)
-    told = jnp.where(last_y, 0.0, jnp.broadcast_to(yr0[near - 1, 4:5, :], (4, 128)))
-    told = [line(jnp.where(lane4 == 4 * (i + 1) + layer, told, 0.0), 1.0) for i in range(4)]
-    ends_y = [jnp.where(is_node, col_mat[n - 1 + i : n + i, :], 0.0) for i in range(2)]
-    late = jnp.concatenate([told[i] * ends_y[0] + told[2 + i] * ends_y[1] for i in range(2)], axis=0)
-    other = other + jnp.concatenate([late, jnp.zeros((32, lanes_c), jnp.float32)], axis=0)
-    lhs = jnp.concatenate([own, c_right, c_left, rest], axis=0).T[0:rows_c]
+    lhs = jnp.concatenate([own, jnp.zeros((8, lanes_c), jnp.float32), rest], axis=0).T[0:rows_c]
     for d in range(DEPTH):
         u1[d] = base[d] + dot(lhs, jnp.where(iota((40, lanes_c), 0) % 4 == d, other, 0.0))
+        w1[d] = detail(u1[d])
 
     n, h, g = n0 // 2, n0 // 4, n0 // 8
     lane = iota((8, 128), 1)
-    for d in range(DEPTH):
-        w1[d] = detail(u1[d])
     ways = jnp.concatenate([rv[8:16, 0:256], row_table("taken")[:, 0:256]], axis=0).T
     functionals = jnp.concatenate([ways[:, 0:2], ways[:, 4:8]], axis=1)
     of_w = dot(row_sums([w1[d] for d in range(DEPTH)], functionals, 6), col_table("mat1"))
@@ -564,9 +573,45 @@
     sent = of_w[0:8] + pltpu.roll(of_second, h + 3, 1)
     for i in range(2):
         sent += pltpu.roll(jnp.where(is_c, of_w[8 + 8 * i : 16 + 8 * i], 0.0), g + 5 + 2 * i, 1)
+    late_rows, late_own = col_table("late"), row_table("late_own")
+    late_ends = [dot(late_own[:, 0:8], late_rows[16 + 8 * i : 24 + 8 * i]) for i in range(2)]
+    late_table = row_table("late")
+
+    pltpu.make_async_copy(yr0, yr0, y_recv.at[0]).wait()
+    ends = []
+    for value in gather(yr0, col_v, col_places, gy_n):
+        tail = line(jnp.where(lane4 == layer, jnp.broadcast_to(value[4:5], (4, 128)), 0.0), 1.0)
+        ends.append(jnp.concatenate([value[0:4], jnp.where(lane4 == 0, tail, 0.0)], axis=1))
+    c_right, c_left = ends
+    c_right += cv[28:29, n0 + 1 : n0 + 2] * (a_right[:, n0 + 1 : n0 + 2] * p_r + a_left[:, n0 + 1 : n0 + 2] * p_l)
+    inner = INNER.get(gy_n, 1)
+    near = inner - 1 + (gy_n - inner) * ((gy % inner + 1) // inner)
+    told = jnp.where(last_y, 0.0, jnp.broadcast_to(yr0[near - 1, 4:5, :], (4, 128)))
+    told = [line(jnp.where(lane4 == 4 * (i + 1) + layer, told, 0.0), 1.0) for i in range(4)]
+    carries = jnp.concatenate([c_right, c_left], axis=0)
+    scalars = dot(carries, late_table)
+    change = []
+    for x_way in range(2):
+        part = jnp.zeros((4, 128), jnp.float32)
+        for m in range(8):
+            for way in range(2):
+                scalar = scalars[4 * way : 4 * way + 4, 2 * m + x_way : 2 * m + x_way + 1]
+                part += scalar * late_rows[8 * way + m : 8 * way + m + 1]
+        for i in range(4):
+            row = 2 * x_way + i % 2
+            part += told[i] * late_ends[i // 2][row : row + 1]
+        change.append(part)
+    sent = sent + jnp.concatenate(change, axis=0)
     xs1[...] = sent
     xr1[0] = sent
     send_same(x_peers, xs1, xr1, x_send.at[1], x_recv.at[1])
+    ends_y = [jnp.where(is_node, col_mat[n0 - 1 + i : n0 + i, :], 0.0) for i in range(2)]
+    late = jnp.concatenate([told[i] * ends_y[0] + told[2 + i] * ends_y[1] for i in range(2)], axis=0)
+    lhs = jnp.concatenate([carries, twice(rv, 2, lanes_c)], axis=0).T[0:rows_c]
+    other = jnp.concatenate([twice(cv, 2, lanes_c), late], axis=0)
+    for d in range(DEPTH):
+        u1[d] = u1[d] + dot(lhs, jnp.where(iota((16, lanes_c), 0) % 4 == d, other, 0.0))
+        w1[d] = detail(u1[d])
     base1, solved1 = local_level(1, n, u1, w1)
     cols = jnp.zeros((padded_rows(h), 128), jnp.float32)
     spot = iota(cols.shape, 1)
@@ -604,6 +649,15 @@
     ys1[...] = sent
     yr1[0] = sent
     send_same(y_peers, ys1, yr1, y_send.at[1], y_recv.at[1])
+    down_turned = jnp.concatenate([col_255, col_255], axis=0).T[0:n0]
+    is_last = iota((n0, 128), 1) == 127
+    for d in range(DEPTH):
+        out_v[d, 0] = w0[d, :, 0:128]
+        out_v[d, 1] = w0[d, :, 128:256] + jnp.where(is_last, down_turned[:, d : d + 1], 0.0)
+        for j in range(2):
+            tail = iota((8, 128), 0) == 7
+            fix = row_255[d : d + 1, 128 * j : 128 * j + 128]
+            out_v[d, j, n0 - 8 : n0, :] = out_v[d, j, n0 - 8 : n0, :] + jnp.where(tail, fix, 0.0)
     base2, _ = local_level(2, h, base1, [detail(base1[d]) for d in range(DEPTH)])
     spread_out([w1[d] for d in range(DEPTH)], n, 256, 2, 2)
     beside = lambda value: jnp.concatenate([value[128 * i : 128 * i + 128] for i in range(3)], axis=1)

time: 35.5 us -> 34.2 us (0.963)
  Pallas kernels: 34.4 us -> 33.2 us
    pallas_call x1, Pallas kernels: 34.4 us -> 33.2 us  [shards(): pl.pallas_call(functools.partial(kernel, gx_n, gy_n, n0, row_places, col_...]
where the time goes in v6:
time: 34.2 us; the launch traced here: 34.1 us
  Pallas kernels  33.2 us (97%)
  local copies, waits for them, and re-layouts  0.97 us (3%)
    pallas_call x1, Pallas kernels, shards(): pl.pallas_call(functools.partial(kernel, gx_n, gy_n, n0, row_places, col_...  33.2 us
    unnamed x1, local copies, waits for them, and re-layouts  0.97 us

profile of v6, /device:TPU:1, one launch (start us, length us, event | category | flops | bytes accessed | tf_op | source)
XLA Modules:
  0.0 34.1 jit_solution(13639886194482251053)
XLA Ops:
  0.0 33.2 %shard_map.37 = f32[4,256,256]{2,1,0:T(8,128)S(1)} custom-call(f32[4,256,256]{2,1,0:T(8,128)} %refs_0_.1, f32[8,1408,128]{2,1,0:T(8,128)} %constant.4.clone.refs_1_, f32[32,1792,128]{2,1,0:T(8,128)} %constant.5.clone.refs_2_), custom_call_target="tpu_custom_call" | custom-call | tf_op jit(solution)/shard_map/pallas_call | solution.py:737
  33.2 1.0 %copy.5 = f32[4,256,256]{2,1,0:T(8,128)} copy(f32[4,256,256]{2,1,0:T(8,128)S(1)} %shard_map.37) | data formatting | bytes 2097152

commit v7 on v6

--- a/solution.py
+++ b/solution.py
@@ -13,7 +13,7 @@
 LENGTH = 64.0
 MESH = pl.DeviceIdType.MESH
 TABLE_LANES = 384
-BEFORE_HALO = 2
+BEFORE_HALO = 3
 INNER = {8: 2, 32: 8}
 VMEM_LIMIT = 52 * 1024 * 1024
 
@@ -386,7 +386,7 @@
         is_tail = iota((rows_c, lanes_c), 0) == h
         for d in range(DEPTH):
             z = dot(row_mat, dot(w[d], col_mat))
-            even = even_rows(tall_v, pick_dot(u[d], select), rows_c)
+            even = pick_dot(even_rows(tall_v, u[d], rows_c), select)
             even = jnp.where(is_tail & last_x, even[h - 2 : h - 1, :], even)
             base.append(jnp.where(iota((rows_c, lanes_c), 1) <= h, z, 0.0) + even)
             solved.append(z)
@@ -555,7 +555,9 @@
     )
     own = jnp.concatenate([twice(rv, 2, lanes_c), twice(rv, 4, lanes_c)], axis=0)
     rest = jnp.concatenate([down_x[8:16], next_col_even, jnp.zeros((4, lanes_c), jnp.float32)], axis=0)
-    lhs = jnp.concatenate([own, jnp.zeros((8, lanes_c), jnp.float32), rest], axis=0).T[0:rows_c]
+    itself = cv[28:29, n0 + 1 : n0 + 2] * (a_right[:, n0 + 1 : n0 + 2] * p_r + a_left[:, n0 + 1 : n0 + 2] * p_l)
+    itself = jnp.concatenate([itself, jnp.zeros((4, lanes_c), jnp.float32)], axis=0)
+    lhs = jnp.concatenate([own, itself, rest], axis=0).T[0:rows_c]
     for d in range(DEPTH):
         u1[d] = base[d] + dot(lhs, jnp.where(iota((40, lanes_c), 0) % 4 == d, other, 0.0))
         w1[d] = detail(u1[d])
@@ -578,18 +580,16 @@
     late_table = row_table("late")
 
     pltpu.make_async_copy(yr0, yr0, y_recv.at[0]).wait()
-    ends = []
-    for value in gather(yr0, col_v, col_places, gy_n):
-        tail = line(jnp.where(lane4 == layer, jnp.broadcast_to(value[4:5], (4, 128)), 0.0), 1.0)
-        ends.append(jnp.concatenate([value[0:4], jnp.where(lane4 == 0, tail, 0.0)], axis=1))
-    c_right, c_left = ends
-    c_right += cv[28:29, n0 + 1 : n0 + 2] * (a_right[:, n0 + 1 : n0 + 2] * p_r + a_left[:, n0 + 1 : n0 + 2] * p_l)
+    values = gather(yr0, col_v, col_places, gy_n)
+    carries = jnp.concatenate([value[0:4] for value in values], axis=0)
+    spot = iota((8, 128), 1) == iota((8, 128), 0) % 4
+    tails = jnp.concatenate([jnp.broadcast_to(value[4:5], (4, 128)) for value in values], axis=0)
+    tails = line(jnp.where(spot, tails, 0.0), 1.0)
     inner = INNER.get(gy_n, 1)
     near = inner - 1 + (gy_n - inner) * ((gy % inner + 1) // inner)
     told = jnp.where(last_y, 0.0, jnp.broadcast_to(yr0[near - 1, 4:5, :], (4, 128)))
     told = [line(jnp.where(lane4 == 4 * (i + 1) + layer, told, 0.0), 1.0) for i in range(4)]
-    carries = jnp.concatenate([c_right, c_left], axis=0)
-    scalars = dot(carries, late_table)
+    scalars = dot(carries, late_table[0:128]) + tails * late_table[128:129]
     change = []
     for x_way in range(2):
         part = jnp.zeros((4, 128), jnp.float32)
@@ -607,6 +607,7 @@
     send_same(x_peers, xs1, xr1, x_send.at[1], x_recv.at[1])
     ends_y = [jnp.where(is_node, col_mat[n0 - 1 + i : n0 + i, :], 0.0) for i in range(2)]
     late = jnp.concatenate([told[i] * ends_y[0] + told[2 + i] * ends_y[1] for i in range(2)], axis=0)
+    carries = jnp.concatenate([carries, jnp.where(lane == 0, tails, 0.0)], axis=1)
     lhs = jnp.concatenate([carries, twice(rv, 2, lanes_c)], axis=0).T[0:rows_c]
     other = jnp.concatenate([twice(cv, 2, lanes_c), late], axis=0)
     for d in range(DEPTH):

time: 34.2 us -> 34.2 us (level)
  no operation moved by 1% of the time
where the time goes in v7:
time: 34.2 us; the launch traced here: 34.1 us
  Pallas kernels  33.1 us (97%)
  local copies, waits for them, and re-layouts  0.97 us (3%)
    pallas_call x1, Pallas kernels, shards(): pl.pallas_call(functools.partial(kernel, gx_n, gy_n, n0, row_places, col_...  33.1 us
    unnamed x1, local copies, waits for them, and re-layouts  0.97 us

profile of v7, /device:TPU:1, one launch (start us, length us, event | category | flops | bytes accessed | tf_op | source)
XLA Modules:
  0.0 34.1 jit_solution(16968236416832596460)
XLA Ops:
  0.0 33.1 %shard_map.37 = f32[4,256,256]{2,1,0:T(8,128)S(1)} custom-call(f32[4,256,256]{2,1,0:T(8,128)} %refs_0_.1, f32[8,1408,128]{2,1,0:T(8,128)} %constant.4.clone.refs_1_, f32[32,1792,128]{2,1,0:T(8,128)} %constant.5.clone.refs_2_), custom_call_target="tpu_custom_call" | custom-call | tf_op jit(solution)/shard_map/pallas_call | solution.py:738
  33.1 1.0 %copy.5 = f32[4,256,256]{2,1,0:T(8,128)} copy(f32[4,256,256]{2,1,0:T(8,128)S(1)} %shard_map.37) | data formatting | bytes 2097152

commit v8 on v6

--- a/solution.py
+++ b/solution.py
@@ -686,7 +686,7 @@
         nodes = base1[d] + dot(lhs1, jnp.where(iota((16, 128), 0) % 4 == d, other1, 0.0))
         details.append(detail(nodes))
     spread_out(details, h, 128, 4, 2)
-    spread_out(last, g, 128, 8, 3)
+    spread_out(last, g, 128, 8, 2)
     for d in range(DEPTH):
         out[d] = jnp.concatenate([out_v[d, j] for j in range(n0 // 128)], axis=1)
 

time: 34.2 us -> 34.2 us (level)
  no operation moved by 1% of the time
where the time goes in v8:
time: 34.2 us; the launch traced here: 34.1 us
  Pallas kernels  33.1 us (97%)
  local copies, waits for them, and re-layouts  0.97 us (3%)
    pallas_call x1, Pallas kernels, shards(): pl.pallas_call(functools.partial(kernel, gx_n, gy_n, n0, row_places, col_...  33.1 us
    unnamed x1, local copies, waits for them, and re-layouts  0.97 us

profile of v8, /device:TPU:1, one launch (start us, length us, event | category | flops | bytes accessed | tf_op | source)
XLA Modules:
  0.0 34.1 jit_solution(16724295295678319383)
XLA Ops:
  0.0 33.1 %shard_map.37 = f32[4,256,256]{2,1,0:T(8,128)S(1)} custom-call(f32[4,256,256]{2,1,0:T(8,128)} %refs_0_.1, f32[8,1408,128]{2,1,0:T(8,128)} %constant.4.clone.refs_1_, f32[32,1792,128]{2,1,0:T(8,128)} %constant.5.clone.refs_2_), custom_call_target="tpu_custom_call" | custom-call | tf_op jit(solution)/shard_map/pallas_call | solution.py:737
  33.2 1.0 %copy.5 = f32[4,256,256]{2,1,0:T(8,128)} copy(f32[4,256,256]{2,1,0:T(8,128)S(1)} %shard_map.37) | data formatting | bytes 2097152
